TPU v7x, 128 devices: a whole 4x4x4 slice. The times are simulated.
128 devices in a mesh: gx: 32 (over x, z_lo, y), gy: 4 (over z_hi, core).
Axes of the slice: x: 4, y: 4, z: 4 (z_hi: 2, z_lo: 2; z = z_hi * 2 + z_lo), core: 2. Of those that a mesh axis runs over, the one named last changes fastest.
Arguments:
- populations: float32 [19, 256, 16384], P(None, 'gx', 'gy'), may hold values from 0 to 1, as said below
- node_cell: int32 [49152, 256], P(('gx', 'gy')), may hold values from 0 to 32767
- node_weight: bfloat16 [49152, 256], P(('gx', 'gy')), may hold values from 0.19921875 to 2
- node_count: int32 [49152], P(('gx', 'gy')), may hold values from 1 to 256, 11010048 in all
- block_brick: int32 [49152, 1], P(('gx', 'gy')), may hold values from 0 to 127; in each aligned block of 384 rows (0 to 383, 384 to 767, ...) at most 4 rows name the same one
Outputs:
- flow_state: float32 [19, 256, 16384], P(None, 'gx', 'gy')
- solid_frac: float32 [256, 16384], P('gx', 'gy')
Inputs may be any that keep to these rules, and one draw needn't show every extreme that they name: `block_brick`: no brick is named by more than 4 of the 384 blocks of one device (aligned blocks of 384 rows); some brick is named by exactly 4 of them. `populations`: each population lies between half and twice its lattice weight w_i.
All inputs are finite; a program needn't handle non-finite values. No bound on the sum of `node_count` on one device may be relied on, other than what follows from the above.
Results may differ from a plain program's by a relative error of at most 0.00095.
Values may be sent and summed in bfloat16 or wider, within the bound.
A program may use at most 192 MiB of HBM per device.

v0:
```python
import jax
import jax.numpy as jnp
import numpy as np
from jax import lax
from jax.sharding import PartitionSpec as P

NZ = 64
STEPS = 3
CAP = 4


lattice_velocities = (
    (0, 0, 0),
    (1, 0, 0),
    (-1, 0, 0),
    (0, 1, 0),
    (0, -1, 0),
    (0, 0, 1),
    (0, 0, -1),
    (1, 1, 0),
    (-1, -1, 0),
    (1, -1, 0),
    (-1, 1, 0),
    (1, 0, 1),
    (-1, 0, -1),
    (1, 0, -1),
    (-1, 0, 1),
    (0, 1, 1),
    (0, -1, -1),
    (0, 1, -1),
    (0, -1, 1),
)
opposite_of = (0, 2, 1, 4, 3, 6, 5, 8, 7, 10, 9, 12, 11, 14, 13, 16, 15, 18, 17)
lattice_weights = (1.0 / 3.0,) + (1.0 / 18.0,) * 6 + (1.0 / 36.0,) * 12
relax_rate = 1.0


def extended(block, sides, width):
    for axis, dim in sides:
        count = lax.axis_size(axis)
        forward = [(i, i + 1) for i in range(count - 1)]
        forward.append((count - 1, 0))
        backward = [(target, source) for source, target in forward]
        low = lax.ppermute(
            lax.slice_in_dim(block, block.shape[dim] - width, None, axis=dim), axis, forward
        )
        high = lax.ppermute(lax.slice_in_dim(block, 0, width, axis=dim), axis, backward)
        block = jnp.concatenate([low, block, high], axis=dim)
    return block


def roll_within(values, offset):
    if offset == 0:
        return values
    z_position = jnp.arange(values.shape[-1]) % NZ
    shifted = jnp.roll(values, offset, axis=-1)
    wrapped = jnp.roll(values, offset - offset * NZ, axis=-1)
    edge_at = 0 if offset > 0 else NZ - 1
    return jnp.where(z_position == edge_at, wrapped, shifted)


def collide(incoming, solid):
    x_dir = jnp.array([entry[0] for entry in lattice_velocities], jnp.float32)[:, None, None]
    y_dir = jnp.array([entry[1] for entry in lattice_velocities], jnp.float32)[:, None, None]
    z_dir = jnp.array([entry[2] for entry in lattice_velocities], jnp.float32)[:, None, None]
    weight_col = jnp.array(lattice_weights, jnp.float32)[:, None, None]
    mass_density = jnp.sum(incoming, axis=0)
    velocity_x = jnp.sum(incoming * x_dir, axis=0) / mass_density
    velocity_y = jnp.sum(incoming * y_dir, axis=0) / mass_density
    velocity_z = jnp.sum(incoming * z_dir, axis=0) / mass_density
    projected = x_dir * velocity_x + y_dir * velocity_y + z_dir * velocity_z
    speed_sq = velocity_x * velocity_x + velocity_y * velocity_y + velocity_z * velocity_z
    equilibrium = (
        weight_col
        * mass_density
        * (1.0 + 3.0 * projected + 4.5 * projected * projected - 1.5 * speed_sq)
    )
    reversed_pops = incoming[np.array(opposite_of)]
    return (1.0 - solid) * (
        incoming + relax_rate * (equilibrium - incoming)
    ) + solid * reversed_pops


def stream_pull(collided):
    extent_x = collided.shape[1]
    extent_yz = collided.shape[2]
    pulled = []
    for number, velocity in enumerate(lattice_velocities):
        shift_x, shift_y, shift_z = velocity
        source = collided[
            number,
            1 - shift_x : extent_x - 1 - shift_x,
            (1 - shift_y) * NZ : extent_yz - (1 + shift_y) * NZ,
        ]
        pulled.append(roll_within(source, shift_z))
    return jnp.stack(pulled)


def rasterize(cells_in, weights_in, bricks, width_x, width_yz):
    block_count = bricks // 8
    cells_rows = cells_in.reshape(block_count, -1)
    weights_rows = weights_in.reshape(block_count, -1)
    high_count = width_x * width_yz // 128

    def add_block(running, members):
        cell_ids, weight_vals = members
        high_part = cell_ids // 128
        low_part = cell_ids % 128
        row_onehot = (
            jnp.arange(high_count, dtype=jnp.int32)[:, None] == high_part[None, :]
        ).astype(jnp.bfloat16)
        col_onehot = jnp.where(
            jnp.arange(128, dtype=jnp.int32)[None, :] == low_part[:, None],
            weight_vals[:, None],
            jnp.zeros((), jnp.bfloat16),
        )
        return (running + jnp.dot(row_onehot, col_onehot, preferred_element_type=jnp.float32), None)

    start_total = jnp.zeros((high_count, 128), jnp.float32)
    density, unused = lax.scan(add_block, start_total, (cells_rows, weights_rows))
    density = density.reshape(width_x, width_yz)
    return density / (1.0 + density)


def on_device(populations, node_cell, node_weight, node_count, block_brick):
    along_x = lax.axis_size("gx")
    along_y = lax.axis_size("gy")
    bricks = along_x * along_y
    node_total = node_cell.shape[1]
    slot_total = bricks * CAP
    target = block_brick[:, 0]
    matches = (target[:, None] == jnp.arange(bricks, dtype=jnp.int32)[None, :]).astype(jnp.int32)
    earlier = jnp.cumsum(matches, axis=0) - matches
    order_rank = jnp.sum(earlier * matches, axis=1)
    slot_index = target * CAP + order_rank
    live_mask = jnp.arange(node_total, dtype=jnp.int32)[None, :] < node_count[:, None]
    masked = jnp.where(live_mask, node_weight, jnp.zeros((), jnp.bfloat16))
    cells_out = jnp.zeros((slot_total, node_total), jnp.int32).at[slot_index].set(node_cell)
    weights_out = jnp.zeros((slot_total, node_total), jnp.bfloat16).at[slot_index].set(masked)
    cells_in, weights_in = (
        lax.all_to_all(cells_out, ("gx", "gy"), split_axis=0, concat_axis=0, tiled=True),
        lax.all_to_all(weights_out, ("gx", "gy"), split_axis=0, concat_axis=0, tiled=True),
    )
    solid_frac = rasterize(cells_in, weights_in, bricks, populations.shape[1], populations.shape[2])
    current = populations
    for repeat in range(STEPS):
        collided = collide(current, solid_frac)
        padded = extended(collided, (("gx", 1),), 1)
        padded = extended(padded, (("gy", 2),), NZ)
        current = stream_pull(padded)
    return (current, solid_frac)


def solution(mesh):
    return jax.shard_map(
        on_device,
        mesh=mesh,
        in_specs=(
            P(None, "gx", "gy"),
            P(("gx", "gy"), None),
            P(("gx", "gy"), None),
            P(("gx", "gy")),
            P(("gx", "gy"), None),
        ),
        out_specs=(P(None, "gx", "gy"), P("gx", "gy")),
        check_vma=False,
    )
```

profile of v0, /device:TPU:1, one launch (start us, length us, event | category | flops | bytes accessed | tf_op | source)
XLA Modules:
  0.0 232.4 jit_solution(9922996675755488462)
XLA Ops:
  6.1 11.5 %all-to-all-start.1 = ((bf16[128,4,256]{2,1,0:T(4,128)(2,1)}), bf16[128,4,256]{2,1,0:T(4,128)(2,1)S(1)}, u32[]{:S(2)}, u32[]{:S(2)}) async-start(bf16[128,4,256]{2,1,0:T(4,128)(2,1)} %all_to_all.14), calls=%async_computation.1 | async-start | bytes 524288 | tf_op jit(solution)/shard_map/all_to_all | solution.py:142
  21.0 7.9 %all-to-all-done.1 = bf16[128,4,256]{2,1,0:T(4,128)(2,1)S(1)} async-done(((bf16[128,4,256]{2,1,0:T(4,128)(2,1)}), bf16[128,4,256]{2,1,0:T(4,128)(2,1)S(1)}, u32[]{:S(2)}, u32[]{:S(2)}) %all-to-all-start.1) | async-done | bytes 262176 | tf_op jit(solution)/shard_map/all_to_all | solution.py:142
  28.9 4.1 %all-to-all-start = ((s32[128,4,256]{2,1,0:T(4,128)}), s32[128,4,256]{2,1,0:T(4,128)S(1)}, u32[]{:S(2)}, u32[]{:S(2)}) async-start(s32[128,4,256]{2,1,0:T(4,128)} %all_to_all.12), calls=%async_computation | async-start | bytes 1048576 | tf_op jit(solution)/shard_map/all_to_all | solution.py:141
  37.5 9.1 %all-to-all-done = s32[128,4,256]{2,1,0:T(4,128)S(1)} async-done(((s32[128,4,256]{2,1,0:T(4,128)}), s32[128,4,256]{2,1,0:T(4,128)S(1)}, u32[]{:S(2)}, u32[]{:S(2)}) %all-to-all-start) | async-done | bytes 524320 | tf_op jit(solution)/shard_map/all_to_all | solution.py:141
  46.9 69.1 %while.13 = (s32[]{:T(128)}, f32[256,128]{1,0:T(8,128)}, s32[16,8192]{1,0:T(8,128)S(1)}, bf16[16,8192]{1,0:T(8,128)(2,1)S(1)}, s32[]{:T(128)}, /*index=5*/s32[]{:T(128)}) while((s32[]{:T(128)}, f32[256,128]{1,0:T(8,128)}, s32[16,8192]{1,0:T(8,128)S(1)}, bf16[16,8192]{1,0:T(8,128)(2,1)S(1)}, s32[]{:T(128)}, ...), condition=%wide.region_6.7_spmd.clone, body=%wide.region_5.6_spmd.clone.sunk | while | flops 541343744 | bytes 540767 | solution.py:120
  47.2 3.2 %fusion.80 = f32[256,128]{1,0:T(8,128)} fusion(s32[8192]{0:T(1024)S(1)} %add_select_fusion.3, s32[8192]{0:T(1024)S(1)} %bitcast.377, bf16[8192]{0:T(1024)(128)(2,1)S(1)} %dynamic-slice_reduce_fusion.2, f32[256,128]{1,0:T(8,128)} %get-tuple-element.235, pred[]{:T(512)S(6)} %compare.13), kind=kOutput, calls=%fused_computation.11.clone.1 | convolution fusion | flops 541130752 | bytes 344065 | tf_op jit(solution)/shard_map/while/body/eval_jaxpr/dot_general | solution.py:117
  50.7 4.1 %fusion.80 = f32[256,128]{1,0:T(8,128)} fusion(s32[8192]{0:T(1024)S(1)} %add_select_fusion.3, s32[8192]{0:T(1024)S(1)} %bitcast.377, bf16[8192]{0:T(1024)(128)(2,1)S(1)} %dynamic-slice_reduce_fusion.2, f32[256,128]{1,0:T(8,128)} %get-tuple-element.235, pred[]{:T(512)S(6)} %compare.13), kind=kOutput, calls=%fused_computation.11.clone.1 | convolution fusion | flops 541130752 | bytes 344065 | tf_op jit(solution)/shard_map/while/body/eval_jaxpr/dot_general | solution.py:117
  55.1 4.1 %fusion.80 = f32[256,128]{1,0:T(8,128)} fusion(s32[8192]{0:T(1024)S(1)} %add_select_fusion.3, s32[8192]{0:T(1024)S(1)} %bitcast.377, bf16[8192]{0:T(1024)(128)(2,1)S(1)} %dynamic-slice_reduce_fusion.2, f32[256,128]{1,0:T(8,128)} %get-tuple-element.235, pred[]{:T(512)S(6)} %compare.13), kind=kOutput, calls=%fused_computation.11.clone.1 | convolution fusion | flops 541130752 | bytes 344065 | tf_op jit(solution)/shard_map/while/body/eval_jaxpr/dot_general | solution.py:117
  59.5 4.1 %fusion.80 = f32[256,128]{1,0:T(8,128)} fusion(s32[8192]{0:T(1024)S(1)} %add_select_fusion.3, s32[8192]{0:T(1024)S(1)} %bitcast.377, bf16[8192]{0:T(1024)(128)(2,1)S(1)} %dynamic-slice_reduce_fusion.2, f32[256,128]{1,0:T(8,128)} %get-tuple-element.235, pred[]{:T(512)S(6)} %compare.13), kind=kOutput, calls=%fused_computation.11.clone.1 | convolution fusion | flops 541130752 | bytes 344065 | tf_op jit(solution)/shard_map/while/body/eval_jaxpr/dot_general | solution.py:117
  63.8 4.1 %fusion.80 = f32[256,128]{1,0:T(8,128)} fusion(s32[8192]{0:T(1024)S(1)} %add_select_fusion.3, s32[8192]{0:T(1024)S(1)} %bitcast.377, bf16[8192]{0:T(1024)(128)(2,1)S(1)} %dynamic-slice_reduce_fusion.2, f32[256,128]{1,0:T(8,128)} %get-tuple-element.235, pred[]{:T(512)S(6)} %compare.13), kind=kOutput, calls=%fused_computation.11.clone.1 | convolution fusion | flops 541130752 | bytes 344065 | tf_op jit(solution)/shard_map/while/body/eval_jaxpr/dot_general | solution.py:117
  68.2 4.1 %fusion.80 = f32[256,128]{1,0:T(8,128)} fusion(s32[8192]{0:T(1024)S(1)} %add_select_fusion.3, s32[8192]{0:T(1024)S(1)} %bitcast.377, bf16[8192]{0:T(1024)(128)(2,1)S(1)} %dynamic-slice_reduce_fusion.2, f32[256,128]{1,0:T(8,128)} %get-tuple-element.235, pred[]{:T(512)S(6)} %compare.13), kind=kOutput, calls=%fused_computation.11.clone.1 | convolution fusion | flops 541130752 | bytes 344065 | tf_op jit(solution)/shard_map/while/body/eval_jaxpr/dot_general | solution.py:117
  72.6 4.1 %fusion.80 = f32[256,128]{1,0:T(8,128)} fusion(s32[8192]{0:T(1024)S(1)} %add_select_fusion.3, s32[8192]{0:T(1024)S(1)} %bitcast.377, bf16[8192]{0:T(1024)(128)(2,1)S(1)} %dynamic-slice_reduce_fusion.2, f32[256,128]{1,0:T(8,128)} %get-tuple-element.235, pred[]{:T(512)S(6)} %compare.13), kind=kOutput, calls=%fused_computation.11.clone.1 | convolution fusion | flops 541130752 | bytes 344065 | tf_op jit(solution)/shard_map/while/body/eval_jaxpr/dot_general | solution.py:117
  76.9 4.1 %fusion.80 = f32[256,128]{1,0:T(8,128)} fusion(s32[8192]{0:T(1024)S(1)} %add_select_fusion.3, s32[8192]{0:T(1024)S(1)} %bitcast.377, bf16[8192]{0:T(1024)(128)(2,1)S(1)} %dynamic-slice_reduce_fusion.2, f32[256,128]{1,0:T(8,128)} %get-tuple-element.235, pred[]{:T(512)S(6)} %compare.13), kind=kOutput, calls=%fused_computation.11.clone.1 | convolution fusion | flops 541130752 | bytes 344065 | tf_op jit(solution)/shard_map/while/body/eval_jaxpr/dot_general | solution.py:117
  81.3 4.1 %fusion.80 = f32[256,128]{1,0:T(8,128)} fusion(s32[8192]{0:T(1024)S(1)} %add_select_fusion.3, s32[8192]{0:T(1024)S(1)} %bitcast.377, bf16[8192]{0:T(1024)(128)(2,1)S(1)} %dynamic-slice_reduce_fusion.2, f32[256,128]{1,0:T(8,128)} %get-tuple-element.235, pred[]{:T(512)S(6)} %compare.13), kind=kOutput, calls=%fused_computation.11.clone.1 | convolution fusion | flops 541130752 | bytes 344065 | tf_op jit(solution)/shard_map/while/body/eval_jaxpr/dot_general | solution.py:117
  85.7 4.1 %fusion.80 = f32[256,128]{1,0:T(8,128)} fusion(s32[8192]{0:T(1024)S(1)} %add_select_fusion.3, s32[8192]{0:T(1024)S(1)} %bitcast.377, bf16[8192]{0:T(1024)(128)(2,1)S(1)} %dynamic-slice_reduce_fusion.2, f32[256,128]{1,0:T(8,128)} %get-tuple-element.235, pred[]{:T(512)S(6)} %compare.13), kind=kOutput, calls=%fused_computation.11.clone.1 | convolution fusion | flops 541130752 | bytes 344065 | tf_op jit(solution)/shard_map/while/body/eval_jaxpr/dot_general | solution.py:117
  90.1 4.1 %fusion.80 = f32[256,128]{1,0:T(8,128)} fusion(s32[8192]{0:T(1024)S(1)} %add_select_fusion.3, s32[8192]{0:T(1024)S(1)} %bitcast.377, bf16[8192]{0:T(1024)(128)(2,1)S(1)} %dynamic-slice_reduce_fusion.2, f32[256,128]{1,0:T(8,128)} %get-tuple-element.235, pred[]{:T(512)S(6)} %compare.13), kind=kOutput, calls=%fused_computation.11.clone.1 | convolution fusion | flops 541130752 | bytes 344065 | tf_op jit(solution)/shard_map/while/body/eval_jaxpr/dot_general | solution.py:117
  94.4 4.1 %fusion.80 = f32[256,128]{1,0:T(8,128)} fusion(s32[8192]{0:T(1024)S(1)} %add_select_fusion.3, s32[8192]{0:T(1024)S(1)} %bitcast.377, bf16[8192]{0:T(1024)(128)(2,1)S(1)} %dynamic-slice_reduce_fusion.2, f32[256,128]{1,0:T(8,128)} %get-tuple-element.235, pred[]{:T(512)S(6)} %compare.13), kind=kOutput, calls=%fused_computation.11.clone.1 | convolution fusion | flops 541130752 | bytes 344065 | tf_op jit(solution)/shard_map/while/body/eval_jaxpr/dot_general | solution.py:117
  98.8 4.1 %fusion.80 = f32[256,128]{1,0:T(8,128)} fusion(s32[8192]{0:T(1024)S(1)} %add_select_fusion.3, s32[8192]{0:T(1024)S(1)} %bitcast.377, bf16[8192]{0:T(1024)(128)(2,1)S(1)} %dynamic-slice_reduce_fusion.2, f32[256,128]{1,0:T(8,128)} %get-tuple-element.235, pred[]{:T(512)S(6)} %compare.13), kind=kOutput, calls=%fused_computation.11.clone.1 | convolution fusion | flops 541130752 | bytes 344065 | tf_op jit(solution)/shard_map/while/body/eval_jaxpr/dot_general | solution.py:117
  103.2 4.1 %fusion.80 = f32[256,128]{1,0:T(8,128)} fusion(s32[8192]{0:T(1024)S(1)} %add_select_fusion.3, s32[8192]{0:T(1024)S(1)} %bitcast.377, bf16[8192]{0:T(1024)(128)(2,1)S(1)} %dynamic-slice_reduce_fusion.2, f32[256,128]{1,0:T(8,128)} %get-tuple-element.235, pred[]{:T(512)S(6)} %compare.13), kind=kOutput, calls=%fused_computation.11.clone.1 | convolution fusion | flops 541130752 | bytes 344065 | tf_op jit(solution)/shard_map/while/body/eval_jaxpr/dot_general | solution.py:117
  107.5 4.1 %fusion.80 = f32[256,128]{1,0:T(8,128)} fusion(s32[8192]{0:T(1024)S(1)} %add_select_fusion.3, s32[8192]{0:T(1024)S(1)} %bitcast.377, bf16[8192]{0:T(1024)(128)(2,1)S(1)} %dynamic-slice_reduce_fusion.2, f32[256,128]{1,0:T(8,128)} %get-tuple-element.235, pred[]{:T(512)S(6)} %compare.13), kind=kOutput, calls=%fused_computation.11.clone.1 | convolution fusion | flops 541130752 | bytes 344065 | tf_op jit(solution)/shard_map/while/body/eval_jaxpr/dot_general | solution.py:117
  111.9 4.1 %fusion.80 = f32[256,128]{1,0:T(8,128)} fusion(s32[8192]{0:T(1024)S(1)} %add_select_fusion.3, s32[8192]{0:T(1024)S(1)} %bitcast.377, bf16[8192]{0:T(1024)(128)(2,1)S(1)} %dynamic-slice_reduce_fusion.2, f32[256,128]{1,0:T(8,128)} %get-tuple-element.235, pred[]{:T(512)S(6)} %compare.13), kind=kOutput, calls=%fused_computation.11.clone.1 | convolution fusion | flops 541130752 | bytes 344065 | tf_op jit(solution)/shard_map/while/body/eval_jaxpr/dot_general | solution.py:117
  117.0 4.2 %fusion.16 = f32[19,8,4096]{2,1,0:T(8,128)S(1)} fusion(f32[19,8,4096]{2,1,0:T(8,128)} %param.25, f32[19,8,4096]{2,1,0:T(8,128)} %gather_fusion, f32[8,4096]{1,0:T(8,128)S(1)} %get-tuple-element.196, f32[8,4096]{1,0:T(8,128)S(1)} %get-tuple-element.132, f32[8,4096]{1,0:T(8,128)S(1)} %get-tuple-element.135, f32[19]{0:T(128)S(1)} %copy-done.80, ...), kind=kLoop, calls=%fused_computation.35 | loop fusion | flops 11206656 | bytes 8388912 | tf_op jit(solution)/shard_map/add | solution.py:79
  123.9 6.3 %collective-permute-done.1 = f32[19,1,4096]{2,1,0:T(1,128)S(1)} collective-permute-done((f32[19,1,4096]{2,1,0:T(1,128)S(1)}, f32[19,1,4096]{2,1,0:T(1,128)S(1)}, u32[]{:S(2)}, u32[]{:S(2)}) %collective-permute-start.1) | collective-permute-done | bytes 311328 | tf_op jit(solution)/shard_map/ppermute | solution.py:47
  130.2 6.1 %collective-permute-done = f32[19,1,4096]{2,1,0:T(1,128)S(1)} collective-permute-done((f32[19,1,4096]{2,1,0:T(1,128)S(1)}, f32[19,1,4096]{2,1,0:T(1,128)S(1)}, u32[]{:S(2)}, u32[]{:S(2)}) %collective-permute-start) | collective-permute-done | bytes 311328 | tf_op jit(solution)/shard_map/ppermute | solution.py:44
  154.3 4.0 %gather_fusion.1 = f32[19,8,4096]{2,1,0:T(8,128)} fusion(f32[19,8,4096]{2,1,0:T(8,128)} %copy-done, s32[1024]{0:T(1024)} %copy-done.91), kind=kCustom, calls=%fused_computation.1 | custom fusion | bytes 4980812 | tf_op jit(solution)/shard_map/gather | solution.py:78
  165.9 5.3 %collective-permute-done.5 = f32[19,1,4096]{2,1,0:T(1,128)S(1)} collective-permute-done((f32[19,1,4096]{2,1,0:T(1,128)S(1)}, f32[19,1,4096]{2,1,0:T(1,128)S(1)}, u32[]{:S(2)}, u32[]{:S(2)}) %collective-permute-start.5) | collective-permute-done | bytes 311328 | tf_op jit(solution)/shard_map/ppermute | solution.py:47
  171.1 5.0 %collective-permute-done.4 = f32[19,1,4096]{2,1,0:T(1,128)S(1)} collective-permute-done((f32[19,1,4096]{2,1,0:T(1,128)S(1)}, f32[19,1,4096]{2,1,0:T(1,128)S(1)}, u32[]{:S(2)}, u32[]{:S(2)}) %collective-permute-start.4) | collective-permute-done | bytes 311328 | tf_op jit(solution)/shard_map/ppermute | solution.py:44
  176.3 3.1 %collective-permute-start.7 = (f32[19,10,64]{2,1,0:T(8,128)S(1)}, f32[19,10,64]{2,1,0:T(8,128)S(1)}, u32[]{:S(2)}, u32[]{:S(2)}) collective-permute-start(f32[19,10,64]{2,1,0:T(8,128)S(1)} %get-tuple-element.160), channel_id=1, source_target_pairs={{1,0},{2,1},{3,2},{0,3},{5,4},{6,5},{7,6},{4,7},{9,8},{10,9},{11,1... | collective-permute-start | bytes 145928 | tf_op jit(solution)/shard_map/ppermute | solution.py:47
  194.8 4.0 %gather_fusion.2 = f32[19,8,4096]{2,1,0:T(8,128)} fusion(f32[19,8,4096]{2,1,0:T(8,128)} %copy-done.2, s32[1024]{0:T(1024)} %copy-done.91), kind=kCustom, calls=%fused_computation.2 | custom fusion | bytes 4980812 | tf_op jit(solution)/shard_map/gather | solution.py:78
  206.4 4.9 %collective-permute-done.9 = f32[19,1,4096]{2,1,0:T(1,128)S(1)} collective-permute-done((f32[19,1,4096]{2,1,0:T(1,128)S(1)}, f32[19,1,4096]{2,1,0:T(1,128)S(1)}, u32[]{:S(2)}, u32[]{:S(2)}) %collective-permute-start.9) | collective-permute-done | bytes 311328 | tf_op jit(solution)/shard_map/ppermute | solution.py:47
  211.3 4.1 %collective-permute-done.8 = f32[19,1,4096]{2,1,0:T(1,128)S(1)} collective-permute-done((f32[19,1,4096]{2,1,0:T(1,128)S(1)}, f32[19,1,4096]{2,1,0:T(1,128)S(1)}, u32[]{:S(2)}, u32[]{:S(2)}) %collective-permute-start.8) | collective-permute-done | bytes 311328 | tf_op jit(solution)/shard_map/ppermute | solution.py:44
  215.5 3.7 %collective-permute-start.11 = (f32[19,10,64]{2,1,0:T(8,128)S(1)}, f32[19,10,64]{2,1,0:T(8,128)S(1)}, u32[]{:S(2)}, u32[]{:S(2)}) collective-permute-start(f32[19,10,64]{2,1,0:T(8,128)S(1)} %get-tuple-element.158), channel_id=1, source_target_pairs={{1,0},{2,1},{3,2},{0,3},{5,4},{6,5},{7,6},{4,7},{9,8},{10,9},{11,1... | collective-permute-start | bytes 145928 | tf_op jit(solution)/shard_map/ppermute | solution.py:47
  (469 shorter events, 82.2 us)
Async XLA Ops:
  1.8 31.2 %copy-start.95 = (s32[19]{0:T(128)S(1)}, s32[19]{0:T(128)}, u32[]{:S(2)}) copy-start(s32[19]{0:T(128)} %constant.214) | copy-start | bytes 232
  1.8 31.2 %copy-start.4 = (f32[19,8,4096]{2,1,0:T(8,128)S(1)}, f32[19,8,4096]{2,1,0:T(8,128)}, u32[]{:S(2)}) copy-start(f32[19,8,4096]{2,1,0:T(8,128)} %param.25) | copy-start | bytes 7471108
  6.1 22.8 %all-to-all-start.1 = ((bf16[128,4,256]{2,1,0:T(4,128)(2,1)}), bf16[128,4,256]{2,1,0:T(4,128)(2,1)S(1)}, u32[]{:S(2)}, u32[]{:S(2)}) async-start(bf16[128,4,256]{2,1,0:T(4,128)(2,1)} %all_to_all.14), calls=%async_computation.1 | async-start | bytes 524288 | tf_op jit(solution)/shard_map/all_to_all | solution.py:142
  28.9 17.7 %all-to-all-start = ((s32[128,4,256]{2,1,0:T(4,128)}), s32[128,4,256]{2,1,0:T(4,128)S(1)}, u32[]{:S(2)}, u32[]{:S(2)}) async-start(s32[128,4,256]{2,1,0:T(4,128)} %all_to_all.12), calls=%async_computation | async-start | bytes 1048576 | tf_op jit(solution)/shard_map/all_to_all | solution.py:141
  46.9 70.0 %copy-start.42 = (f32[8,4096]{1,0:T(8,128)S(1)}, f32[8,4096]{1,0:T(8,128)}, u32[]{:S(2)}) copy-start(f32[8,4096]{1,0:T(8,128)} %get-tuple-element.81) | copy-start | bytes 393220
  46.9 70.0 %copy-start.43 = (f32[8,4096]{1,0:T(8,128)S(1)}, f32[8,4096]{1,0:T(8,128)}, u32[]{:S(2)}) copy-start(f32[8,4096]{1,0:T(8,128)} %get-tuple-element.82) | copy-start | bytes 393220
  117.0 85.4 %copy-start.7 = (f32[8,4096]{1,0:T(8,128)}, f32[8,4096]{1,0:T(8,128)S(1)}, u32[]{:S(2)}) copy-start(f32[8,4096]{1,0:T(8,128)S(1)} %get-tuple-element.196) | copy-start | bytes 393220
  121.8 8.4 %collective-permute-start.1 = (f32[19,1,4096]{2,1,0:T(1,128)S(1)}, f32[19,1,4096]{2,1,0:T(1,128)S(1)}, u32[]{:S(2)}, u32[]{:S(2)}) collective-permute-start(f32[19,1,4096]{2,1,0:T(1,128)S(1)} %get-tuple-element.187), channel_id=1, source_target_pairs={{4,0},{8,4},{12,8},{16,12},{20,16},{24,20},{28,24},{32,28},{36,32}... | collective-permute-start | bytes 933896 | tf_op jit(solution)/shard_map/ppermute | solution.py:47
  123.9 12.4 %collective-permute-start = (f32[19,1,4096]{2,1,0:T(1,128)S(1)}, f32[19,1,4096]{2,1,0:T(1,128)S(1)}, u32[]{:S(2)}, u32[]{:S(2)}) collective-permute-start(f32[19,1,4096]{2,1,0:T(1,128)S(1)} %get-tuple-element.188), channel_id=1, source_target_pairs={{0,4},{4,8},{8,12},{12,16},{16,20},{20,24},{24,28},{28,32},{32,36}... | collective-permute-start | bytes 933896 | tf_op jit(solution)/shard_map/ppermute | solution.py:44
  136.4 7.3 %collective-permute-start.3 = (f32[19,10,64]{2,1,0:T(8,128)S(1)}, f32[19,10,64]{2,1,0:T(8,128)S(1)}, u32[]{:S(2)}, u32[]{:S(2)}) collective-permute-start(f32[19,10,64]{2,1,0:T(8,128)S(1)} %get-tuple-element.162), channel_id=1, source_target_pairs={{1,0},{2,1},{3,2},{0,3},{5,4},{6,5},{7,6},{4,7},{9,8},{10,9},{11,1... | collective-permute-start | bytes 145928 | tf_op jit(solution)/shard_map/ppermute | solution.py:47
  138.1 4.0 %collective-permute-start.2 = (f32[19,10,64]{2,1,0:T(8,128)S(1)}, f32[19,10,64]{2,1,0:T(8,128)S(1)}, u32[]{:S(2)}, u32[]{:S(2)}) collective-permute-start(f32[19,10,64]{2,1,0:T(8,128)S(1)} %get-tuple-element.163), channel_id=1, source_target_pairs={{0,1},{1,2},{2,3},{3,0},{4,5},{5,6},{6,7},{7,4},{8,9},{9,10},{10,1... | collective-permute-start | bytes 145928 | tf_op jit(solution)/shard_map/ppermute | solution.py:44
  149.9 3.1 %copy-start.81 = (f32[19]{0:T(128)S(1)}, f32[19]{0:T(128)}, u32[]{:S(2)}) copy-start(f32[19]{0:T(128)} %constant.208.clone) | copy-start | bytes 232
  158.3 3.7 %copy-start.1 = (f32[19,8,4096]{2,1,0:T(8,128)S(1)}, f32[19,8,4096]{2,1,0:T(8,128)}, u32[]{:S(2)}) copy-start(f32[19,8,4096]{2,1,0:T(8,128)} %copy-done) | copy-start | bytes 7471108
  158.3 3.7 %copy-start.6 = (f32[19,8,4096]{2,1,0:T(8,128)S(1)}, f32[19,8,4096]{2,1,0:T(8,128)}, u32[]{:S(2)}) copy-start(f32[19,8,4096]{2,1,0:T(8,128)} %gather_fusion.1) | copy-start | bytes 7471108
  158.3 3.7 %copy-start.82 = (f32[19]{0:T(128)S(1)}, f32[19]{0:T(128)}, u32[]{:S(2)}) copy-start(f32[19]{0:T(128)} %constant.208.clone) | copy-start | bytes 232
  158.3 3.7 %copy-start.86 = (f32[19]{0:T(128)S(1)}, f32[19]{0:T(128)}, u32[]{:S(2)}) copy-start(f32[19]{0:T(128)} %constant.207.clone) | copy-start | bytes 232
  158.3 3.7 %copy-start.89 = (f32[19]{0:T(128)S(1)}, f32[19]{0:T(128)}, u32[]{:S(2)}) copy-start(f32[19]{0:T(128)} %constant.206.clone) | copy-start | bytes 232
  158.3 3.7 %copy-start.93 = (f32[19]{0:T(128)S(1)}, f32[19]{0:T(128)}, u32[]{:S(2)}) copy-start(f32[19]{0:T(128)} %constant.209.clone) | copy-start | bytes 232
  164.3 6.8 %collective-permute-start.5 = (f32[19,1,4096]{2,1,0:T(1,128)S(1)}, f32[19,1,4096]{2,1,0:T(1,128)S(1)}, u32[]{:S(2)}, u32[]{:S(2)}) collective-permute-start(f32[19,1,4096]{2,1,0:T(1,128)S(1)} %get-tuple-element.183), channel_id=1, source_target_pairs={{4,0},{8,4},{12,8},{16,12},{20,16},{24,20},{28,24},{32,28},{36,32}... | collective-permute-start | bytes 933896 | tf_op jit(solution)/shard_map/ppermute | solution.py:47
  165.1 11.0 %collective-permute-start.4 = (f32[19,1,4096]{2,1,0:T(1,128)S(1)}, f32[19,1,4096]{2,1,0:T(1,128)S(1)}, u32[]{:S(2)}, u32[]{:S(2)}) collective-permute-start(f32[19,1,4096]{2,1,0:T(1,128)S(1)} %get-tuple-element.184), channel_id=1, source_target_pairs={{0,4},{4,8},{8,12},{12,16},{16,20},{20,24},{24,28},{28,32},{32,36}... | collective-permute-start | bytes 933896 | tf_op jit(solution)/shard_map/ppermute | solution.py:44
  176.3 7.9 %collective-permute-start.7 = (f32[19,10,64]{2,1,0:T(8,128)S(1)}, f32[19,10,64]{2,1,0:T(8,128)S(1)}, u32[]{:S(2)}, u32[]{:S(2)}) collective-permute-start(f32[19,10,64]{2,1,0:T(8,128)S(1)} %get-tuple-element.160), channel_id=1, source_target_pairs={{1,0},{2,1},{3,2},{0,3},{5,4},{6,5},{7,6},{4,7},{9,8},{10,9},{11,1... | collective-permute-start | bytes 145928 | tf_op jit(solution)/shard_map/ppermute | solution.py:47
  179.4 4.0 %collective-permute-start.6 = (f32[19,10,64]{2,1,0:T(8,128)S(1)}, f32[19,10,64]{2,1,0:T(8,128)S(1)}, u32[]{:S(2)}, u32[]{:S(2)}) collective-permute-start(f32[19,10,64]{2,1,0:T(8,128)S(1)} %get-tuple-element.161), channel_id=1, source_target_pairs={{0,1},{1,2},{2,3},{3,0},{4,5},{5,6},{6,7},{7,4},{8,9},{9,10},{10,1... | collective-permute-start | bytes 145928 | tf_op jit(solution)/shard_map/ppermute | solution.py:44
  198.7 3.7 %copy-start.3 = (f32[19,8,4096]{2,1,0:T(8,128)S(1)}, f32[19,8,4096]{2,1,0:T(8,128)}, u32[]{:S(2)}) copy-start(f32[19,8,4096]{2,1,0:T(8,128)} %copy-done.2) | copy-start | bytes 7471108
  198.7 3.7 %copy-start.5 = (f32[19,8,4096]{2,1,0:T(8,128)S(1)}, f32[19,8,4096]{2,1,0:T(8,128)}, u32[]{:S(2)}) copy-start(f32[19,8,4096]{2,1,0:T(8,128)} %gather_fusion.2) | copy-start | bytes 7471108
  198.7 3.7 %copy-start.83 = (f32[19]{0:T(128)S(1)}, f32[19]{0:T(128)}, u32[]{:S(2)}) copy-start(f32[19]{0:T(128)} %constant.208.clone) | copy-start | bytes 232
  198.8 3.7 %copy-start.87 = (f32[19]{0:T(128)S(1)}, f32[19]{0:T(128)}, u32[]{:S(2)}) copy-start(f32[19]{0:T(128)} %constant.207.clone) | copy-start | bytes 232
  198.8 3.7 %copy-start.90 = (f32[19]{0:T(128)S(1)}, f32[19]{0:T(128)}, u32[]{:S(2)}) copy-start(f32[19]{0:T(128)} %constant.206.clone) | copy-start | bytes 232
  198.8 3.7 %copy-start.94 = (f32[19]{0:T(128)S(1)}, f32[19]{0:T(128)}, u32[]{:S(2)}) copy-start(f32[19]{0:T(128)} %constant.209.clone) | copy-start | bytes 232
  204.8 6.5 %collective-permute-start.9 = (f32[19,1,4096]{2,1,0:T(1,128)S(1)}, f32[19,1,4096]{2,1,0:T(1,128)S(1)}, u32[]{:S(2)}, u32[]{:S(2)}) collective-permute-start(f32[19,1,4096]{2,1,0:T(1,128)S(1)} %get-tuple-element.179), channel_id=1, source_target_pairs={{4,0},{8,4},{12,8},{16,12},{20,16},{24,20},{28,24},{32,28},{36,32}... | collective-permute-start | bytes 933896 | tf_op jit(solution)/shard_map/ppermute | solution.py:47
  204.9 10.5 %collective-permute-start.8 = (f32[19,1,4096]{2,1,0:T(1,128)S(1)}, f32[19,1,4096]{2,1,0:T(1,128)S(1)}, u32[]{:S(2)}, u32[]{:S(2)}) collective-permute-start(f32[19,1,4096]{2,1,0:T(1,128)S(1)} %get-tuple-element.180), channel_id=1, source_target_pairs={{0,4},{4,8},{8,12},{12,16},{16,20},{20,24},{24,28},{28,32},{32,36}... | collective-permute-start | bytes 933896 | tf_op jit(solution)/shard_map/ppermute | solution.py:44
  215.5 11.4 %collective-permute-start.11 = (f32[19,10,64]{2,1,0:T(8,128)S(1)}, f32[19,10,64]{2,1,0:T(8,128)S(1)}, u32[]{:S(2)}, u32[]{:S(2)}) collective-permute-start(f32[19,10,64]{2,1,0:T(8,128)S(1)} %get-tuple-element.158), channel_id=1, source_target_pairs={{1,0},{2,1},{3,2},{0,3},{5,4},{6,5},{7,6},{4,7},{9,8},{10,9},{11,1... | collective-permute-start | bytes 145928 | tf_op jit(solution)/shard_map/ppermute | solution.py:47
  219.3 5.0 %collective-permute-start.10 = (f32[19,10,64]{2,1,0:T(8,128)S(1)}, f32[19,10,64]{2,1,0:T(8,128)S(1)}, u32[]{:S(2)}, u32[]{:S(2)}) collective-permute-start(f32[19,10,64]{2,1,0:T(8,128)S(1)} %get-tuple-element.159), channel_id=1, source_target_pairs={{0,1},{1,2},{2,3},{3,0},{4,5},{5,6},{6,7},{7,4},{8,9},{9,10},{10,1... | collective-permute-start | bytes 145928 | tf_op jit(solution)/shard_map/ppermute | solution.py:44
  (78 other events, 135.9 us)
where the time goes:
time: 233 us; the launch traced here: 232 us
  matrix products  64 us (27%)
  waiting for transfers between devices  56.4 us (24%)
  other arithmetic  44.7 us (19%)
  starting transfers between devices  35.1 us (15%)
  local copies, waits for them, and re-layouts  29.3 us (13%)
  between operations  2.68 us (1%)
    dot_general x16, matrix products, add_block(): jnp.dot(row_onehot, col_onehot, preferred_element_type=jnp.float32)  64 us
    ppermute x6, waiting for transfers between devices, extended(): lax.ppermute(lax.slice_in_dim(block, 0, width, axis=dim), axis, backward)  19.8 us
    ppermute x6, waiting for transfers between devices, extended(): lax.ppermute(lax.slice_in_dim(block, block.shape[dim] - width, None, axis...  19.5 us
    unnamed x46, other arithmetic  13.2 us
    all_to_all x1, starting transfers between devices, on_device(): lax.all_to_all(weights_out, ('gx', 'gy'), split_axis=0, concat_axis=0, ti...  11.5 us
    ppermute x6, starting transfers between devices, extended(): lax.ppermute(lax.slice_in_dim(block, 0, width, axis=dim), axis, backward)  11.3 us
    gather x3, local copies, waits for them, and re-layouts, collide(): reversed_pops = incoming[np.array(opposite_of)]  10.1 us
    all_to_all x1, waiting for transfers between devices, on_device(): lax.all_to_all(cells_out, ('gx', 'gy'), split_axis=0, concat_axis=0, tile...  9.12 us
  transfers between devices with their start and end apart: 14, of which 13 were waited for; matrix products, arithmetic and copies ran while one was open for 5% of the time, Pallas kernels for 0%

commit v1 on v0

--- a/solution.py
+++ b/solution.py
@@ -1,12 +1,23 @@
+import functools
+
 import jax
 import jax.numpy as jnp
 import numpy as np
 from jax import lax
+from jax.experimental import pallas as pl
+from jax.experimental.pallas import tpu as pltpu
 from jax.sharding import PartitionSpec as P
 
 NZ = 64
 STEPS = 3
 CAP = 4
+LANES = 128
+GROUP = 8
+CHUNK = 16
+WEIGHT_STEPS = 1024.0
+REST_SCALE = 64.0
+MESH = pl.DeviceIdType.MESH
+NARROW = jnp.float8_e4m3fn
 
 
 lattice_velocities = (
@@ -96,52 +107,183 @@
     return jnp.stack(pulled)
 
 
-def rasterize(cells_in, weights_in, bricks, width_x, width_yz):
-    block_count = bricks // 8
-    cells_rows = cells_in.reshape(block_count, -1)
-    weights_rows = weights_in.reshape(block_count, -1)
-    high_count = width_x * width_yz // 128
-
-    def add_block(running, members):
-        cell_ids, weight_vals = members
-        high_part = cell_ids // 128
-        low_part = cell_ids % 128
-        row_onehot = (
-            jnp.arange(high_count, dtype=jnp.int32)[:, None] == high_part[None, :]
-        ).astype(jnp.bfloat16)
-        col_onehot = jnp.where(
-            jnp.arange(128, dtype=jnp.int32)[None, :] == low_part[:, None],
-            weight_vals[:, None],
-            jnp.zeros((), jnp.bfloat16),
+def brick_slots(me, bricks, target_ref, count_ref, cell_ref, weight_ref, operand):
+    blocks, nodes = cell_ref.shape
+    row = lax.broadcasted_iota(jnp.int32, (blocks, blocks), 0)
+    col = lax.broadcasted_iota(jnp.int32, (blocks, blocks), 1)
+    target_col = target_ref[...]
+    brick = lax.broadcasted_iota(jnp.int32, (blocks, bricks), 1)
+    matches = jnp.where(brick == target_col, 1.0, 0.0)
+    before = jnp.where(col < row, 1.0, 0.0).astype(jnp.bfloat16)
+    earlier = jnp.dot(before, matches.astype(jnp.bfloat16), preferred_element_type=jnp.float32)
+    rank = jnp.sum(earlier * matches, axis=1, keepdims=True)
+    slot_col = target_col.astype(jnp.float32) * CAP + rank
+    slot_row = jnp.sum(jnp.where(row == col, slot_col, 0.0), axis=0, keepdims=True)
+    count_row = count_ref[...].astype(jnp.float32)
+    count_col = jnp.sum(jnp.where(row == col, count_row, 0.0), axis=1, keepdims=True)
+    node = lax.broadcasted_iota(jnp.int32, (blocks, nodes), 1).astype(jnp.float32)
+    live = node < count_col
+    cell = cell_ref[...]
+    high = ((cell >> 7) & 31) * 8 + (cell >> 12)
+    low = cell & 127
+    weight = jnp.where(live, weight_ref[...].astype(jnp.float32), 0.0)
+    for part in range(2):
+        lanes = slice(part * LANES, (part + 1) * LANES)
+        for number, values in enumerate((high.astype(jnp.float32), low.astype(jnp.float32), weight)):
+            at = (part * 3 + number) * LANES
+            operand[:, at : at + LANES] = values[:, lanes].astype(jnp.bfloat16)
+    return slot_row
+
+
+def send_chunk(me, bricks, along_y, chunk, slot_row, operand, outgoing, arrived, sent_sem, arrived_sem):
+    rows = CHUNK * 8
+    place = lax.broadcasted_iota(jnp.int32, (rows, 1), 0)
+    offset = chunk * CHUNK + (place >> 3)
+    wanted = lax.rem(me + offset, bricks) * CAP + (place & (CAP - 1))
+    pick = jnp.where(wanted.astype(jnp.float32) == slot_row, 1.0, 0.0).astype(jnp.bfloat16)
+    found = jnp.dot(pick, operand[...], preferred_element_type=jnp.float32)
+    lower = (place & 7) < CAP
+    high, low, weight = [
+        jnp.where(
+            lower,
+            found[:, number * LANES : (number + 1) * LANES],
+            found[:, (3 + number) * LANES : (4 + number) * LANES],
         )
-        return (running + jnp.dot(row_onehot, col_onehot, preferred_element_type=jnp.float32), None)
-
-    start_total = jnp.zeros((high_count, 128), jnp.float32)
-    density, unused = lax.scan(add_block, start_total, (cells_rows, weights_rows))
-    density = density.reshape(width_x, width_yz)
-    return density / (1.0 + density)
+        for number in range(3)
+    ]
+    packed = ((weight * WEIGHT_STEPS).astype(jnp.int32) << 15) + (high * LANES + low).astype(jnp.int32)
+    base = pl.multiple_of(chunk * CHUNK, CHUNK)
+    outgoing[pl.ds(base, CHUNK)] = packed.reshape(CHUNK, 8, LANES)
+
+    def start(place_in, carry):
+        step = base + place_in
+        target = lax.rem(me + step, bricks)
+
+        @pl.when(step > 0)
+        def _():
+            pltpu.make_async_remote_copy(
+                src_ref=outgoing.at[step],
+                dst_ref=arrived.at[step],
+                send_sem=sent_sem,
+                recv_sem=arrived_sem.at[step // GROUP],
+                device_id=(target // along_y, lax.rem(target, along_y)),
+                device_id_type=MESH,
+            ).start()
+
+        return carry
+
+    lax.fori_loop(0, CHUNK, start, 0)
+
+
+def one_hots(values, line):
+    node = values[line : line + 1, :]
+    high = (node >> 7) & 255
+    low = node & 127
+    weight = (node >> 15).astype(jnp.float32) * (1.0 / WEIGHT_STEPS)
+    coarse = weight.astype(NARROW).astype(jnp.float32)
+    rest = (weight - coarse) * REST_SCALE
+
+    def wide(entry):
+        return jnp.broadcast_to(entry.astype(jnp.float32), (16, LANES)).astype(jnp.bfloat16)
+
+    high, low, coarse, rest = wide(high), wide(low), wide(coarse), wide(rest)
+    counting = lax.broadcasted_iota(jnp.int32, (16, LANES), 0).astype(jnp.float32)
+    one, zero = jnp.ones((16, LANES), jnp.bfloat16), jnp.zeros((16, LANES), jnp.bfloat16)
+    rows, first, second = [], [], []
+    for part in range(16):
+        rows.append(jnp.where(high == (counting + 16 * part).astype(jnp.bfloat16), one, zero))
+    for part in range(8):
+        hit = low == (counting + 16 * part).astype(jnp.bfloat16)
+        first.append(jnp.where(hit, coarse, zero))
+        second.append(jnp.where(hit, rest, zero))
+    return (
+        jnp.concatenate(rows, 0).astype(NARROW),
+        jnp.concatenate(first + second, 0).astype(NARROW),
+    )
+
+
+def raster_kernel(
+    bricks, along_y, target_ref, count_ref, cell_ref, weight_ref, solid_ref,
+    operand, outgoing, arrived, total, sent_sem, arrived_sem,
+):
+    me = lax.axis_index("gx") * along_y + lax.axis_index("gy")
+    slot_row = brick_slots(me, bricks, target_ref, count_ref, cell_ref, weight_ref, operand)
+    total[...] = jnp.zeros_like(total)
+
+    def send(chunk, carry):
+        send_chunk(
+            me, bricks, along_y, chunk, slot_row, operand, outgoing, arrived, sent_sem, arrived_sem
+        )
+        return carry
+
+    lax.fori_loop(0, bricks // CHUNK, send, 0)
+    arrived[0] = outgoing[0]
+
+    def add(group):
+        left, right = [], []
+        for member in range(GROUP):
+            values = arrived[group * GROUP + member]
+            for line in range(8):
+                rows, columns = one_hots(values, line)
+                left.append(rows)
+                right.append(columns)
+        total[...] += lax.dot_general(
+            jnp.concatenate(left, 1),
+            jnp.concatenate(right, 1),
+            (((1,), (1,)), ((), ())),
+            preferred_element_type=jnp.float32,
+        )
+
+    def landed(group, skip):
+        whole = arrived.at[pl.ds(group * GROUP + skip, GROUP - skip)]
+        pltpu.make_async_copy(whole, whole, arrived_sem.at[group]).wait()
+
+    def later(group, carry):
+        @pl.when(group == 0)
+        def _():
+            landed(0, 1)
+
+        @pl.when(group > 0)
+        def _():
+            landed(group, 0)
+
+        add(group)
+        return carry
+
+    lax.fori_loop(0, bricks // GROUP, later, 0)
+    everything = outgoing.at[pl.ds(1, bricks - 1)]
+    pltpu.make_async_copy(everything, everything, sent_sem).wait()
+    density = total[:, :LANES] + total[:, LANES:] * (1.0 / REST_SCALE)
+    solid_ref[...] = density / (1.0 + density)
+
+
+def rasterize(block_brick, node_count, node_cell, node_weight, bricks, along_y):
+    blocks, nodes = node_cell.shape
+    return pl.pallas_call(
+        functools.partial(raster_kernel, bricks, along_y),
+        out_shape=jax.ShapeDtypeStruct((256, LANES), jnp.float32),
+        in_specs=[pl.BlockSpec(memory_space=pltpu.VMEM)] * 4,
+        out_specs=pl.BlockSpec(memory_space=pltpu.VMEM),
+        scratch_shapes=[
+            pltpu.VMEM((blocks, 6 * LANES), jnp.bfloat16),
+            pltpu.VMEM((bricks, 8, LANES), jnp.int32),
+            pltpu.VMEM((bricks, 8, LANES), jnp.int32),
+            pltpu.VMEM((256, 2 * LANES), jnp.float32),
+            pltpu.SemaphoreType.DMA,
+            pltpu.SemaphoreType.DMA((bricks // GROUP,)),
+        ],
+        compiler_params=pltpu.CompilerParams(
+            has_side_effects=True, vmem_limit_bytes=48 * 1024 * 1024
+        ),
+        name="rasterize",
+    )(block_brick, node_count.reshape(1, blocks), node_cell, node_weight)
 
 
 def on_device(populations, node_cell, node_weight, node_count, block_brick):
-    along_x = lax.axis_size("gx")
     along_y = lax.axis_size("gy")
-    bricks = along_x * along_y
-    node_total = node_cell.shape[1]
-    slot_total = bricks * CAP
-    target = block_brick[:, 0]
-    matches = (target[:, None] == jnp.arange(bricks, dtype=jnp.int32)[None, :]).astype(jnp.int32)
-    earlier = jnp.cumsum(matches, axis=0) - matches
-    order_rank = jnp.sum(earlier * matches, axis=1)
-    slot_index = target * CAP + order_rank
-    live_mask = jnp.arange(node_total, dtype=jnp.int32)[None, :] < node_count[:, None]
-    masked = jnp.where(live_mask, node_weight, jnp.zeros((), jnp.bfloat16))
-    cells_out = jnp.zeros((slot_total, node_total), jnp.int32).at[slot_index].set(node_cell)
-    weights_out = jnp.zeros((slot_total, node_total), jnp.bfloat16).at[slot_index].set(masked)
-    cells_in, weights_in = (
-        lax.all_to_all(cells_out, ("gx", "gy"), split_axis=0, concat_axis=0, tiled=True),
-        lax.all_to_all(weights_out, ("gx", "gy"), split_axis=0, concat_axis=0, tiled=True),
-    )
-    solid_frac = rasterize(cells_in, weights_in, bricks, populations.shape[1], populations.shape[2])
+    bricks = lax.axis_size("gx") * along_y
+    solid = rasterize(block_brick, node_count, node_cell, node_weight, bricks, along_y)
+    solid_frac = solid.reshape(32, 8, LANES).transpose(1, 0, 2).reshape(8, 32 * LANES)
     current = populations
     for repeat in range(STEPS):
         collided = collide(current, solid_frac)

time: 233 us -> 159 us (0.68)
  matrix products: 64 us -> 0 us
  Pallas kernels: 0 us -> 35.7 us
  waiting for transfers between devices: 56.4 us -> 35 us
  starting transfers between devices: 35.1 us -> 23.8 us
  other arithmetic: 44.7 us -> 35.8 us
  local copies, waits for them, and re-layouts: 29.3 us -> 25.6 us
    dot_general x16 -> x0, matrix products: 64 us -> none  [add_block(): jnp.dot(row_onehot, col_onehot, preferred_element_type=jnp.float32)]
    pallas_call x0 -> x1, Pallas kernels: none -> 35.7 us  [rasterize(): pl.pallas_call(functools.partial(raster_kernel, bricks, along_y), out_sha...]
    all_to_all x2 -> x0, waiting for transfers between devices: 17 us -> none  [the longest x1 9.12 us: on_device(): lax.all_to_all(cells_out, ('gx', 'gy'), split_axis=0, concat_axis=0, tile...]
    all_to_all x2 -> x0, starting transfers between devices: 15.6 us -> none  [the longest x1 11.5 us: on_device(): lax.all_to_all(weights_out, ('gx', 'gy'), split_axis=0, concat_axis=0, ti...]
    ppermute x6, starting transfers between devices: 11.3 us -> 18.7 us  [extended(): lax.ppermute(lax.slice_in_dim(block, 0, width, axis=dim), axis, backward)]
    ppermute x6, waiting for transfers between devices: 19.8 us -> 13.1 us  [extended(): lax.ppermute(lax.slice_in_dim(block, 0, width, axis=dim), axis, backward)]
    select_n x33 -> x0, other arithmetic: 3.82 us -> none  [the longest x16 2.71 us: add_block(): high_part = cell_ids // 128]
    ppermute x6, starting transfers between devices: 8.18 us -> 5.05 us  [extended(): lax.ppermute(lax.slice_in_dim(block, block.shape[dim] - width, None, axis...]
  transfers between devices with their start and end apart: 14 -> 12, of which waited for: 13 -> 9; matrix products, arithmetic and copies ran while one was open for 5% -> 3% of each run, Pallas kernels for 0% -> 0%
where the time goes in v1:
time: 159 us
  other arithmetic  35.8 us (23%)
  Pallas kernels  35.7 us (22%)
  waiting for transfers between devices  35 us (22%)
  local copies, waits for them, and re-layouts  25.6 us (16%)
  starting transfers between devices  23.8 us (15%)
  between operations  2.67 us (2%)
    pallas_call x1, Pallas kernels, rasterize(): pl.pallas_call(functools.partial(raster_kernel, bricks, along_y), out_sha...  35.7 us
    ppermute x6, waiting for transfers between devices, extended(): lax.ppermute(lax.slice_in_dim(block, block.shape[dim] - width, None, axis...  21.9 us
    ppermute x6, starting transfers between devices, extended(): lax.ppermute(lax.slice_in_dim(block, 0, width, axis=dim), axis, backward)  18.7 us
    ppermute x6, waiting for transfers between devices, extended(): lax.ppermute(lax.slice_in_dim(block, 0, width, axis=dim), axis, backward)  13.1 us
    unnamed x44, other arithmetic  12.4 us
    gather x3, local copies, waits for them, and re-layouts, collide(): reversed_pops = incoming[np.array(opposite_of)]  11.9 us
    mul x4, other arithmetic, collide(): projected = x_dir * velocity_x + y_dir * velocity_y + z_dir * velocity_z  7.23 us
    add x3, other arithmetic, collide(): (1.0 - solid) * (incoming + relax_rate * (equilibrium - incoming))  7.01 us
  transfers between devices with their start and end apart: 12, of which 9 were waited for; matrix products, arithmetic and copies ran while one was open for 3% of the time, Pallas kernels for 0%

profile of v1, /device:TPU:1, one launch (start us, length us, event | category | flops | bytes accessed | tf_op | source)
XLA Modules:
  0.0 158.6 jit_solution(128705669237525602)
XLA Ops:
  2.8 4.0 %gather_fusion = f32[19,8,4096]{2,1,0:T(8,128)} fusion(f32[19,8,4096]{2,1,0:T(8,128)} %param.23, s32[1024]{0:T(1024)S(1)} %pad_clamp_fusion), kind=kCustom, calls=%fused_computation | custom fusion | bytes 4980812 | tf_op jit(solution)/shard_map/gather | solution.py:89
  7.9 35.7 %rasterize.1 = f32[256,128]{1,0:T(8,128)S(1)} custom-call(s32[384,1]{1,0:T(8,128)S(1)} %copy.56.target_ref, s32[1,384]{1,0:T(1,128)S(1)} %reshape.3201.count_ref, s32[384,256]{1,0:T(8,128)S(1)} %copy-done, bf16[384,256]{1,0:T(8,128)(2,1)S(1)} %copy-done.1), custom_call_target="tpu_custom_call" | custom-call | tf_op jit(solution)/shard_map/rasterize/pallas_call | solution.py:262
  43.8 3.5 %fusion.4 = f32[19,8,4096]{2,1,0:T(8,128)S(1)} fusion(f32[19,8,4096]{2,1,0:T(8,128)S(1)} %copy-done.7, f32[19,8,4096]{2,1,0:T(8,128)} %gather_fusion, f32[8,4096]{1,0:T(8,128)S(1)} %bitcast.360, f32[8,4096]{1,0:T(8,128)S(1)} %get-tuple-element.48, f32[8,4096]{1,0:T(8,128)S(1)} %get-tuple-element.51, f32[19]{0:T(128)S(1)} %copy-done.86, ...), kind=kLoop, calls=%fused_computation.13 | loop fusion | flops 11206656 | bytes 8388912 | tf_op jit(solution)/shard_map/add | solution.py:90
  48.6 5.1 %collective-permute-start.1 = (f32[19,1,4096]{2,1,0:T(1,128)S(1)}, f32[19,1,4096]{2,1,0:T(1,128)S(1)}, u32[]{:S(2)}, u32[]{:S(2)}) collective-permute-start(f32[19,1,4096]{2,1,0:T(1,128)S(1)} %get-tuple-element.103), channel_id=1, source_target_pairs={{4,0},{8,4},{12,8},{16,12},{20,16},{24,20},{28,24},{32,28},{36,32}... | collective-permute-start | bytes 933896 | tf_op jit(solution)/shard_map/ppermute | solution.py:58
  53.7 6.9 %collective-permute-done = f32[19,1,4096]{2,1,0:T(1,128)S(1)} collective-permute-done((f32[19,1,4096]{2,1,0:T(1,128)S(1)}, f32[19,1,4096]{2,1,0:T(1,128)S(1)}, u32[]{:S(2)}, u32[]{:S(2)}) %collective-permute-start) | collective-permute-done | bytes 311328 | tf_op jit(solution)/shard_map/ppermute | solution.py:55
  60.8 2.3 %collective-permute-start.2 = (f32[19,10,64]{2,1,0:T(8,128)S(1)}, f32[19,10,64]{2,1,0:T(8,128)S(1)}, u32[]{:S(2)}, u32[]{:S(2)}) collective-permute-start(f32[19,10,64]{2,1,0:T(8,128)S(1)} %get-tuple-element.79), channel_id=1, source_target_pairs={{0,1},{1,2},{2,3},{3,0},{4,5},{5,6},{6,7},{7,4},{8,9},{9,10},{10,1... | collective-permute-start | bytes 145928 | tf_op jit(solution)/shard_map/ppermute | solution.py:55
  66.0 3.3 %collective-permute-done.3 = f32[19,10,64]{2,1,0:T(8,128)S(1)} collective-permute-done((f32[19,10,64]{2,1,0:T(8,128)S(1)}, f32[19,10,64]{2,1,0:T(8,128)S(1)}, u32[]{:S(2)}, u32[]{:S(2)}) %collective-permute-start.3) | collective-permute-done | bytes 48672 | tf_op jit(solution)/shard_map/ppermute | solution.py:58
  72.3 0.9 fusion.23
  73.5 0.9 fusion.24
  77.2 1.4 copy-done.2
  78.6 1.3 multiply_reduce_fusion.3
  79.9 4.0 %gather_fusion.1 = f32[19,8,4096]{2,1,0:T(8,128)} fusion(f32[19,8,4096]{2,1,0:T(8,128)} %copy-done.2, s32[1024]{0:T(1024)} %copy-done.90), kind=kCustom, calls=%fused_computation.1 | custom fusion | bytes 4980812 | tf_op jit(solution)/shard_map/gather | solution.py:89
  83.9 2.6 %fusion.42 = (f32[8,4096]{1,0:T(8,128)S(1)}, f32[1,8,4096]{2,1,0:T(8,128)S(1)}) fusion(f32[8,4096]{1,0:T(8,128)S(1)} %get-tuple-element.7, f32[1,8,4095]{2,1,0:T(8,128)} %copy-done.38, f32[1,8,1]{2,1,0:T(8,128)} %copy-done.76, f32[1,8,63]{2,1,0:T(8,128)} %copy-done.77, f32[1,8,4033]{2,1,0:T(8,128)} %copy-done.39, f32[1,8,1]{2,1,0:T(8,128)} %copy-done.72, ...), kind=kLoop, calls=%fused_computation.339 | loop fusion | flops 1605632 | bytes 4202496 | tf_op jit(solution)/shard_map/mul | solution.py:82
  86.6 1.0 fusion.43
  87.6 1.8 %fusion.9 = f32[19,8,4096]{2,1,0:T(8,128)S(1)} fusion(f32[19,8,4096]{2,1,0:T(8,128)S(1)} %copy-done.3, f32[19,8,4096]{2,1,0:T(8,128)S(1)} %copy-done.9, f32[8,4096]{1,0:T(8,128)S(1)} %get-tuple-element.109, f32[8,4096]{1,0:T(8,128)S(1)} %get-tuple-element.110, f32[8,4096]{1,0:T(8,128)S(1)} %get-tuple-element.108, f32[8,4096]{1,0:T(8,128)S(1)} %get-tuple-element.30, ...), kind=kLoop, calls=%fused_computation.18 | loop fusion | flops 11206656 | bytes 8388912 | tf_op jit(solution)/shard_map/add | solution.py:90
  90.1 5.8 %collective-permute-start.5 = (f32[19,1,4096]{2,1,0:T(1,128)S(1)}, f32[19,1,4096]{2,1,0:T(1,128)S(1)}, u32[]{:S(2)}, u32[]{:S(2)}) collective-permute-start(f32[19,1,4096]{2,1,0:T(1,128)S(1)} %get-tuple-element.99), channel_id=1, source_target_pairs={{4,0},{8,4},{12,8},{16,12},{20,16},{24,20},{28,24},{32,28},{36,32}... | collective-permute-start | bytes 933896 | tf_op jit(solution)/shard_map/ppermute | solution.py:58
  95.9 7.1 %collective-permute-done.4 = f32[19,1,4096]{2,1,0:T(1,128)S(1)} collective-permute-done((f32[19,1,4096]{2,1,0:T(1,128)S(1)}, f32[19,1,4096]{2,1,0:T(1,128)S(1)}, u32[]{:S(2)}, u32[]{:S(2)}) %collective-permute-start.4) | collective-permute-done | bytes 311328 | tf_op jit(solution)/shard_map/ppermute | solution.py:55
  103.2 1.0 collective-permute-start.6
  107.1 4.5 %collective-permute-done.7 = f32[19,10,64]{2,1,0:T(8,128)S(1)} collective-permute-done((f32[19,10,64]{2,1,0:T(8,128)S(1)}, f32[19,10,64]{2,1,0:T(8,128)S(1)}, u32[]{:S(2)}, u32[]{:S(2)}) %collective-permute-start.7) | collective-permute-done | bytes 48672 | tf_op jit(solution)/shard_map/ppermute | solution.py:58
  114.7 0.9 fusion.19
  115.8 0.9 fusion.20
  119.5 1.4 copy-done.4
  120.9 1.3 multiply_reduce_fusion
  122.2 4.0 %gather_fusion.2 = f32[19,8,4096]{2,1,0:T(8,128)} fusion(f32[19,8,4096]{2,1,0:T(8,128)} %copy-done.4, s32[1024]{0:T(1024)} %copy-done.90), kind=kCustom, calls=%fused_computation.2 | custom fusion | bytes 4980812 | tf_op jit(solution)/shard_map/gather | solution.py:89
  126.2 2.6 %fusion.45 = (f32[8,4096]{1,0:T(8,128)S(1)}, f32[1,8,4096]{2,1,0:T(8,128)S(1)}) fusion(f32[8,4096]{1,0:T(8,128)S(1)} %get-tuple-element.4, f32[1,8,4095]{2,1,0:T(8,128)} %copy-done.36, f32[1,8,1]{2,1,0:T(8,128)} %copy-done.74, f32[1,8,63]{2,1,0:T(8,128)} %copy-done.75, f32[1,8,4033]{2,1,0:T(8,128)} %copy-done.37, f32[1,8,1]{2,1,0:T(8,128)} %copy-done.70, ...), kind=kLoop, calls=%fused_computation.342 | loop fusion | flops 1605632 | bytes 4202496 | tf_op jit(solution)/shard_map/mul | solution.py:82
  128.9 1.0 fusion.46
  129.9 1.8 %fusion.14 = f32[19,8,4096]{2,1,0:T(8,128)S(1)} fusion(f32[19,8,4096]{2,1,0:T(8,128)S(1)} %copy-done.5, f32[19,8,4096]{2,1,0:T(8,128)S(1)} %copy-done.8, f32[8,4096]{1,0:T(8,128)S(1)} %get-tuple-element.106, f32[8,4096]{1,0:T(8,128)S(1)} %get-tuple-element.107, f32[8,4096]{1,0:T(8,128)S(1)} %get-tuple-element.105, f32[8,4096]{1,0:T(8,128)S(1)} %get-tuple-element.12, ...), kind=kLoop, calls=%fused_computation.23 | loop fusion | flops 11206656 | bytes 8388912 | tf_op jit(solution)/shard_map/add | solution.py:90
  132.4 5.8 %collective-permute-start.9 = (f32[19,1,4096]{2,1,0:T(1,128)S(1)}, f32[19,1,4096]{2,1,0:T(1,128)S(1)}, u32[]{:S(2)}, u32[]{:S(2)}) collective-permute-start(f32[19,1,4096]{2,1,0:T(1,128)S(1)} %get-tuple-element.95), channel_id=1, source_target_pairs={{4,0},{8,4},{12,8},{16,12},{20,16},{24,20},{28,24},{32,28},{36,32}... | collective-permute-start | bytes 933896 | tf_op jit(solution)/shard_map/ppermute | solution.py:58
  138.2 6.2 %collective-permute-done.8 = f32[19,1,4096]{2,1,0:T(1,128)S(1)} collective-permute-done((f32[19,1,4096]{2,1,0:T(1,128)S(1)}, f32[19,1,4096]{2,1,0:T(1,128)S(1)}, u32[]{:S(2)}, u32[]{:S(2)}) %collective-permute-start.8) | collective-permute-done | bytes 311328 | tf_op jit(solution)/shard_map/ppermute | solution.py:55
  144.5 0.9 collective-permute-start.10
  145.5 1.4 collective-permute-start.11
  147.8 5.3 %collective-permute-done.11 = f32[19,10,64]{2,1,0:T(8,128)S(1)} collective-permute-done((f32[19,10,64]{2,1,0:T(8,128)S(1)}, f32[19,10,64]{2,1,0:T(8,128)S(1)}, u32[]{:S(2)}, u32[]{:S(2)}) %collective-permute-start.11) | collective-permute-done | bytes 48672 | tf_op jit(solution)/shard_map/ppermute | solution.py:58
  (385 shorter events, 29.3 us)
Async XLA Ops:
  2.8 4.0 %copy-start.90 = (s32[1024]{0:T(1024)}, s32[1024]{0:T(1024)S(1)}, u32[]{:S(2)}) copy-start(s32[1024]{0:T(1024)S(1)} %pad_clamp_fusion) | copy-start | bytes 12292
  2.8 4.0 %copy-start.6 = (f32[19,8,4096]{2,1,0:T(8,128)S(1)}, f32[19,8,4096]{2,1,0:T(8,128)}, u32[]{:S(2)}) copy-start(f32[19,8,4096]{2,1,0:T(8,128)} %param.23) | copy-start | bytes 7471108
  2.8 4.0 %copy-start.78 = (f32[19]{0:T(128)S(1)}, f32[19]{0:T(128)}, u32[]{:S(2)}) copy-start(f32[19]{0:T(128)} %constant.130.clone) | copy-start | bytes 232
  2.8 4.0 %copy-start.82 = (f32[19]{0:T(128)S(1)}, f32[19]{0:T(128)}, u32[]{:S(2)}) copy-start(f32[19]{0:T(128)} %constant.131.clone) | copy-start | bytes 232
  2.8 4.0 %copy-start.86 = (f32[19]{0:T(128)S(1)}, f32[19]{0:T(128)}, u32[]{:S(2)}) copy-start(f32[19]{0:T(128)} %constant.132.clone) | copy-start | bytes 232
  6.9 36.8 %copy-start.7 = (f32[19,8,4096]{2,1,0:T(8,128)S(1)}, f32[19,8,4096]{2,1,0:T(8,128)}, u32[]{:S(2)}) copy-start(f32[19,8,4096]{2,1,0:T(8,128)} %param.23) | copy-start | bytes 7471108
  6.9 36.8 %copy-start.92 = (f32[19]{0:T(128)S(1)}, f32[19]{0:T(128)}, u32[]{:S(2)}) copy-start(f32[19]{0:T(128)} %constant.133.clone) | copy-start | bytes 232
  47.9 12.7 %collective-permute-start = (f32[19,1,4096]{2,1,0:T(1,128)S(1)}, f32[19,1,4096]{2,1,0:T(1,128)S(1)}, u32[]{:S(2)}, u32[]{:S(2)}) collective-permute-start(f32[19,1,4096]{2,1,0:T(1,128)S(1)} %get-tuple-element.104), channel_id=1, source_target_pairs={{0,4},{4,8},{8,12},{12,16},{16,20},{20,24},{24,28},{28,32},{32,36}... | collective-permute-start | bytes 933896 | tf_op jit(solution)/shard_map/ppermute | solution.py:55
  48.6 12.0 %collective-permute-start.1 = (f32[19,1,4096]{2,1,0:T(1,128)S(1)}, f32[19,1,4096]{2,1,0:T(1,128)S(1)}, u32[]{:S(2)}, u32[]{:S(2)}) collective-permute-start(f32[19,1,4096]{2,1,0:T(1,128)S(1)} %get-tuple-element.103), channel_id=1, source_target_pairs={{4,0},{8,4},{12,8},{16,12},{20,16},{24,20},{28,24},{32,28},{36,32}... | collective-permute-start | bytes 933896 | tf_op jit(solution)/shard_map/ppermute | solution.py:58
  60.8 4.5 %collective-permute-start.2 = (f32[19,10,64]{2,1,0:T(8,128)S(1)}, f32[19,10,64]{2,1,0:T(8,128)S(1)}, u32[]{:S(2)}, u32[]{:S(2)}) collective-permute-start(f32[19,10,64]{2,1,0:T(8,128)S(1)} %get-tuple-element.79), channel_id=1, source_target_pairs={{0,1},{1,2},{2,3},{3,0},{4,5},{5,6},{6,7},{7,4},{8,9},{9,10},{10,1... | collective-permute-start | bytes 145928 | tf_op jit(solution)/shard_map/ppermute | solution.py:55
  63.1 6.2 %collective-permute-start.3 = (f32[19,10,64]{2,1,0:T(8,128)S(1)}, f32[19,10,64]{2,1,0:T(8,128)S(1)}, u32[]{:S(2)}, u32[]{:S(2)}) collective-permute-start(f32[19,10,64]{2,1,0:T(8,128)S(1)} %get-tuple-element.78), channel_id=1, source_target_pairs={{1,0},{2,1},{3,2},{0,3},{5,4},{6,5},{7,6},{4,7},{9,8},{10,9},{11,1... | collective-permute-start | bytes 145928 | tf_op jit(solution)/shard_map/ppermute | solution.py:58
  75.2 3.4 %copy-start.79 = (f32[19]{0:T(128)S(1)}, f32[19]{0:T(128)}, u32[]{:S(2)}) copy-start(f32[19]{0:T(128)} %constant.130.clone) | copy-start | bytes 232
  83.9 3.7 %copy-start.3 = (f32[19,8,4096]{2,1,0:T(8,128)S(1)}, f32[19,8,4096]{2,1,0:T(8,128)}, u32[]{:S(2)}) copy-start(f32[19,8,4096]{2,1,0:T(8,128)} %copy-done.2) | copy-start | bytes 7471108
  83.9 3.7 %copy-start.9 = (f32[19,8,4096]{2,1,0:T(8,128)S(1)}, f32[19,8,4096]{2,1,0:T(8,128)}, u32[]{:S(2)}) copy-start(f32[19,8,4096]{2,1,0:T(8,128)} %gather_fusion.1) | copy-start | bytes 7471108
  83.9 3.7 %copy-start.80 = (f32[19]{0:T(128)S(1)}, f32[19]{0:T(128)}, u32[]{:S(2)}) copy-start(f32[19]{0:T(128)} %constant.130.clone) | copy-start | bytes 232
  83.9 3.7 %copy-start.84 = (f32[19]{0:T(128)S(1)}, f32[19]{0:T(128)}, u32[]{:S(2)}) copy-start(f32[19]{0:T(128)} %constant.131.clone) | copy-start | bytes 232
  83.9 3.7 %copy-start.88 = (f32[19]{0:T(128)S(1)}, f32[19]{0:T(128)}, u32[]{:S(2)}) copy-start(f32[19]{0:T(128)} %constant.132.clone) | copy-start | bytes 232
  83.9 3.7 %copy-start.93 = (f32[19]{0:T(128)S(1)}, f32[19]{0:T(128)}, u32[]{:S(2)}) copy-start(f32[19]{0:T(128)} %constant.133.clone) | copy-start | bytes 232
  90.0 13.0 %collective-permute-start.4 = (f32[19,1,4096]{2,1,0:T(1,128)S(1)}, f32[19,1,4096]{2,1,0:T(1,128)S(1)}, u32[]{:S(2)}, u32[]{:S(2)}) collective-permute-start(f32[19,1,4096]{2,1,0:T(1,128)S(1)} %get-tuple-element.100), channel_id=1, source_target_pairs={{0,4},{4,8},{8,12},{12,16},{16,20},{20,24},{24,28},{28,32},{32,36}... | collective-permute-start | bytes 933896 | tf_op jit(solution)/shard_map/ppermute | solution.py:55
  90.1 12.9 %collective-permute-start.5 = (f32[19,1,4096]{2,1,0:T(1,128)S(1)}, f32[19,1,4096]{2,1,0:T(1,128)S(1)}, u32[]{:S(2)}, u32[]{:S(2)}) collective-permute-start(f32[19,1,4096]{2,1,0:T(1,128)S(1)} %get-tuple-element.99), channel_id=1, source_target_pairs={{4,0},{8,4},{12,8},{16,12},{20,16},{24,20},{28,24},{32,28},{36,32}... | collective-permute-start | bytes 933896 | tf_op jit(solution)/shard_map/ppermute | solution.py:58
  103.2 3.2 %collective-permute-start.6 = (f32[19,10,64]{2,1,0:T(8,128)S(1)}, f32[19,10,64]{2,1,0:T(8,128)S(1)}, u32[]{:S(2)}, u32[]{:S(2)}) collective-permute-start(f32[19,10,64]{2,1,0:T(8,128)S(1)} %get-tuple-element.77), channel_id=1, source_target_pairs={{0,1},{1,2},{2,3},{3,0},{4,5},{5,6},{6,7},{7,4},{8,9},{9,10},{10,1... | collective-permute-start | bytes 145928 | tf_op jit(solution)/shard_map/ppermute | solution.py:55
  104.2 7.5 %collective-permute-start.7 = (f32[19,10,64]{2,1,0:T(8,128)S(1)}, f32[19,10,64]{2,1,0:T(8,128)S(1)}, u32[]{:S(2)}, u32[]{:S(2)}) collective-permute-start(f32[19,10,64]{2,1,0:T(8,128)S(1)} %get-tuple-element.76), channel_id=1, source_target_pairs={{1,0},{2,1},{3,2},{0,3},{5,4},{6,5},{7,6},{4,7},{9,8},{10,9},{11,1... | collective-permute-start | bytes 145928 | tf_op jit(solution)/shard_map/ppermute | solution.py:58
  126.2 3.7 %copy-start.5 = (f32[19,8,4096]{2,1,0:T(8,128)S(1)}, f32[19,8,4096]{2,1,0:T(8,128)}, u32[]{:S(2)}) copy-start(f32[19,8,4096]{2,1,0:T(8,128)} %copy-done.4) | copy-start | bytes 7471108
  126.2 3.7 %copy-start.8 = (f32[19,8,4096]{2,1,0:T(8,128)S(1)}, f32[19,8,4096]{2,1,0:T(8,128)}, u32[]{:S(2)}) copy-start(f32[19,8,4096]{2,1,0:T(8,128)} %gather_fusion.2) | copy-start | bytes 7471108
  126.2 3.7 %copy-start.81 = (f32[19]{0:T(128)S(1)}, f32[19]{0:T(128)}, u32[]{:S(2)}) copy-start(f32[19]{0:T(128)} %constant.130.clone) | copy-start | bytes 232
  126.2 3.7 %copy-start.85 = (f32[19]{0:T(128)S(1)}, f32[19]{0:T(128)}, u32[]{:S(2)}) copy-start(f32[19]{0:T(128)} %constant.131.clone) | copy-start | bytes 232
  126.2 3.7 %copy-start.89 = (f32[19]{0:T(128)S(1)}, f32[19]{0:T(128)}, u32[]{:S(2)}) copy-start(f32[19]{0:T(128)} %constant.132.clone) | copy-start | bytes 232
  126.2 3.7 %copy-start.94 = (f32[19]{0:T(128)S(1)}, f32[19]{0:T(128)}, u32[]{:S(2)}) copy-start(f32[19]{0:T(128)} %constant.133.clone) | copy-start | bytes 232
  132.3 12.1 %collective-permute-start.8 = (f32[19,1,4096]{2,1,0:T(1,128)S(1)}, f32[19,1,4096]{2,1,0:T(1,128)S(1)}, u32[]{:S(2)}, u32[]{:S(2)}) collective-permute-start(f32[19,1,4096]{2,1,0:T(1,128)S(1)} %get-tuple-element.96), channel_id=1, source_target_pairs={{0,4},{4,8},{8,12},{12,16},{16,20},{20,24},{24,28},{28,32},{32,36}... | collective-permute-start | bytes 933896 | tf_op jit(solution)/shard_map/ppermute | solution.py:55
  132.4 12.0 %collective-permute-start.9 = (f32[19,1,4096]{2,1,0:T(1,128)S(1)}, f32[19,1,4096]{2,1,0:T(1,128)S(1)}, u32[]{:S(2)}, u32[]{:S(2)}) collective-permute-start(f32[19,1,4096]{2,1,0:T(1,128)S(1)} %get-tuple-element.95), channel_id=1, source_target_pairs={{4,0},{8,4},{12,8},{16,12},{20,16},{24,20},{28,24},{32,28},{36,32}... | collective-permute-start | bytes 933896 | tf_op jit(solution)/shard_map/ppermute | solution.py:58
  144.5 3.1 %collective-permute-start.10 = (f32[19,10,64]{2,1,0:T(8,128)S(1)}, f32[19,10,64]{2,1,0:T(8,128)S(1)}, u32[]{:S(2)}, u32[]{:S(2)}) collective-permute-start(f32[19,10,64]{2,1,0:T(8,128)S(1)} %get-tuple-element.75), channel_id=1, source_target_pairs={{0,1},{1,2},{2,3},{3,0},{4,5},{5,6},{6,7},{7,4},{8,9},{9,10},{10,1... | collective-permute-start | bytes 145928 | tf_op jit(solution)/shard_map/ppermute | solution.py:55
  145.5 7.6 %collective-permute-start.11 = (f32[19,10,64]{2,1,0:T(8,128)S(1)}, f32[19,10,64]{2,1,0:T(8,128)S(1)}, u32[]{:S(2)}, u32[]{:S(2)}) collective-permute-start(f32[19,10,64]{2,1,0:T(8,128)S(1)} %get-tuple-element.74), channel_id=1, source_target_pairs={{1,0},{2,1},{3,2},{0,3},{5,4},{6,5},{7,6},{4,7},{9,8},{10,9},{11,1... | collective-permute-start | bytes 145928 | tf_op jit(solution)/shard_map/ppermute | solution.py:58
  (75 other events, 132.4 us)

commit v2 on v1

--- a/solution.py
+++ b/solution.py
@@ -43,68 +43,236 @@
 )
 opposite_of = (0, 2, 1, 4, 3, 6, 5, 8, 7, 10, 9, 12, 11, 14, 13, 16, 15, 18, 17)
 lattice_weights = (1.0 / 3.0,) + (1.0 / 18.0,) * 6 + (1.0 / 36.0,) * 12
-relax_rate = 1.0
-
-
-def extended(block, sides, width):
-    for axis, dim in sides:
-        count = lax.axis_size(axis)
-        forward = [(i, i + 1) for i in range(count - 1)]
-        forward.append((count - 1, 0))
-        backward = [(target, source) for source, target in forward]
-        low = lax.ppermute(
-            lax.slice_in_dim(block, block.shape[dim] - width, None, axis=dim), axis, forward
+
+
+ROWS = 32
+TOP = 8
+TALL = 48
+POPS = 19
+RIGHT = (1, 7, 9, 11, 13)
+LEFT = (2, 8, 10, 12, 14)
+UP = (3, 7, 10, 15, 17)
+DOWN = (4, 8, 9, 16, 18)
+
+
+def place_of_lane():
+    lane = lax.broadcasted_iota(jnp.int32, (8, LANES), 1)
+    return lane < NZ, (lane & (NZ - 1)) == 0, (lane & (NZ - 1)) == NZ - 1
+
+
+def pull(post, number, plane, tile):
+    shift_x, shift_y, shift_z = lattice_velocities[number]
+    even, z_first, z_last = place_of_lane()
+    base = TOP + 8 * tile
+    values = post[plane + 1 - shift_x, number, base : base + 8, :]
+    turn = 0
+    if shift_y == 1:
+        values = jnp.where(even, values, post[plane + 1 - shift_x, number, base - 1 : base + 7, :])
+        turn = NZ
+    if shift_y == -1:
+        values = jnp.where(even, post[plane + 1 - shift_x, number, base + 1 : base + 9, :], values)
+        turn = NZ
+    if shift_z == 0:
+        return pltpu.roll(values, turn, 1) if turn else values
+    near = pltpu.roll(values, (shift_z + turn) % LANES, 1)
+    wrapped = pltpu.roll(values, (shift_z - shift_z * NZ + turn) % LANES, 1)
+    return jnp.where(z_first if shift_z == 1 else z_last, wrapped, near)
+
+
+def collide(f, solid):
+    pairs = range(1, POPS, 2)
+    sums = {i: f[i] + f[i + 1] for i in pairs}
+    diffs = {i: f[i] - f[i + 1] for i in pairs}
+    rho = f[0] + ((sums[1] + sums[3]) + (sums[5] + sums[7])) + (
+        ((sums[9] + sums[11]) + (sums[13] + sums[15])) + sums[17]
+    )
+    jx = (diffs[1] + diffs[7]) + (diffs[9] + diffs[11]) + diffs[13]
+    jy = (diffs[3] + diffs[7]) + (diffs[15] + diffs[17]) - diffs[9]
+    jz = (diffs[5] + diffs[11]) + (diffs[15] - diffs[13]) - diffs[17]
+    fluid = 1.0 - solid
+    inverse = 1.0 / rho
+    ux, uy, uz = jx * inverse, jy * inverse, jz * inverse
+    jx, jy, jz = jx * fluid, jy * fluid, jz * fluid
+    xx, yy, zz = jx * ux, jy * uy, jz * uz
+    base = rho * fluid - 1.5 * (xx + yy + zz)
+    hx, hy, hz = jx * (1.0 / 12.0), jy * (1.0 / 12.0), jz * (1.0 / 12.0)
+    vx, vy, vz = ux * 1.5, uy * 1.5, uz * 1.5
+    base_axis, base_diagonal = base * (1.0 / 18.0), base * (1.0 / 36.0)
+    post = [base * (1.0 / 3.0) + solid * f[0]] + [None] * 18
+
+    def put(i, even, odd):
+        post[i] = (even + odd) + solid * f[i + 1]
+        post[i + 1] = (even - odd) + solid * f[i]
+
+    for i, square, h in ((1, xx, hx), (3, yy, hy), (5, zz, hz)):
+        put(i, base_axis + 0.25 * square, 2.0 * h)
+    for i, h, v in (
+        (7, hx + hy, vx + vy),
+        (9, hx - hy, vx - vy),
+        (11, hx + hz, vx + vz),
+        (13, hx - hz, vx - vz),
+        (15, hy + hz, vy + vz),
+        (17, hy - hz, vy - vz),
+    ):
+        put(i, base_diagonal + h * v, h)
+    return post
+
+
+def lattice(start, solid, result, result_out, posts, x_send, x_recv, y_send, y_recv, c_send, c_recv, sent, came, out_sem):
+    here_x, here_y = lax.axis_index("gx"), lax.axis_index("gy")
+    along_x, along_y = lax.axis_size("gx"), lax.axis_size("gy")
+    ahead_x, behind_x = lax.rem(here_x + 1, along_x), lax.rem(here_x + along_x - 1, along_x)
+    ahead_y, behind_y = lax.rem(here_y + 1, along_y), lax.rem(here_y + along_y - 1, along_y)
+    partners = (
+        (ahead_x, here_y),
+        (behind_x, here_y),
+        (here_x, ahead_y),
+        (here_x, behind_y),
+        (ahead_x, ahead_y),
+        (behind_x, behind_y),
+        (ahead_x, behind_y),
+        (behind_x, ahead_y),
+    )
+    first, last = TOP, TOP + ROWS - 1
+
+    def copy(step, way):
+        if way < 2:
+            source, landing = x_send.at[step, way], x_recv.at[step, way]
+        elif way < 4:
+            source, landing = y_send.at[step, way - 2], y_recv.at[step, way - 2]
+        else:
+            source, landing = c_send.at[step, way - 4], c_recv.at[step, way - 4]
+        return pltpu.make_async_remote_copy(
+            src_ref=source,
+            dst_ref=landing,
+            send_sem=sent.at[step, way],
+            recv_sem=came.at[step, way],
+            device_id=partners[way],
+            device_id_type=MESH,
         )
-        high = lax.ppermute(lax.slice_in_dim(block, 0, width, axis=dim), axis, backward)
-        block = jnp.concatenate([low, block, high], axis=dim)
-    return block
-
-
-def roll_within(values, offset):
-    if offset == 0:
-        return values
-    z_position = jnp.arange(values.shape[-1]) % NZ
-    shifted = jnp.roll(values, offset, axis=-1)
-    wrapped = jnp.roll(values, offset - offset * NZ, axis=-1)
-    edge_at = 0 if offset > 0 else NZ - 1
-    return jnp.where(z_position == edge_at, wrapped, shifted)
-
-
-def collide(incoming, solid):
-    x_dir = jnp.array([entry[0] for entry in lattice_velocities], jnp.float32)[:, None, None]
-    y_dir = jnp.array([entry[1] for entry in lattice_velocities], jnp.float32)[:, None, None]
-    z_dir = jnp.array([entry[2] for entry in lattice_velocities], jnp.float32)[:, None, None]
-    weight_col = jnp.array(lattice_weights, jnp.float32)[:, None, None]
-    mass_density = jnp.sum(incoming, axis=0)
-    velocity_x = jnp.sum(incoming * x_dir, axis=0) / mass_density
-    velocity_y = jnp.sum(incoming * y_dir, axis=0) / mass_density
-    velocity_z = jnp.sum(incoming * z_dir, axis=0) / mass_density
-    projected = x_dir * velocity_x + y_dir * velocity_y + z_dir * velocity_z
-    speed_sq = velocity_x * velocity_x + velocity_y * velocity_y + velocity_z * velocity_z
-    equilibrium = (
-        weight_col
-        * mass_density
-        * (1.0 + 3.0 * projected + 4.5 * projected * projected - 1.5 * speed_sq)
-    )
-    reversed_pops = incoming[np.array(opposite_of)]
-    return (1.0 - solid) * (
-        incoming + relax_rate * (equilibrium - incoming)
-    ) + solid * reversed_pops
-
-
-def stream_pull(collided):
-    extent_x = collided.shape[1]
-    extent_yz = collided.shape[2]
-    pulled = []
-    for number, velocity in enumerate(lattice_velocities):
-        shift_x, shift_y, shift_z = velocity
-        source = collided[
-            number,
-            1 - shift_x : extent_x - 1 - shift_x,
-            (1 - shift_y) * NZ : extent_yz - (1 + shift_y) * NZ,
-        ]
-        pulled.append(roll_within(source, shift_z))
-    return jnp.stack(pulled)
+
+    def send_x(step, post):
+        for way, plane, group in ((0, 8, RIGHT), (1, 1, LEFT)):
+            for place, number in enumerate(group):
+                for half in range(2):
+                    values = post[plane, number, first + 16 * half : first + 16 * half + 16, :]
+                    at = place * ROWS + 16 * half
+                    x_send[step, way, at : at + 16, :] = values.astype(jnp.bfloat16)
+            copy(step, way).start()
+        for way, number, plane, row in ((4, 7, 8, last - 7), (5, 8, 1, first), (6, 9, 8, first), (7, 10, 1, last - 7)):
+            c_send[step, way - 4] = post[plane, number, row : row + 8, :]
+            copy(step, way).start()
+
+    def send_y(step, post):
+        for way, row, group in ((2, last, UP), (3, first, DOWN)):
+            for place, number in enumerate(group):
+                for plane in range(8):
+                    at = place * 8 + plane
+                    y_send[step, way - 2, at : at + 1, :] = post[plane + 1, number, row : row + 1, :]
+            copy(step, way).start()
+
+    def receive(step, post):
+        for way in range(8):
+            copy(step, way).wait_recv()
+        for way, plane, group in ((0, 0, RIGHT), (1, 9, LEFT)):
+            for place, number in enumerate(group):
+                for half in range(2):
+                    at = place * ROWS + 16 * half
+                    values = x_recv[step, way, at : at + 16, :]
+                    post[plane, number, first + 16 * half : first + 16 * half + 16, :] = values.astype(jnp.float32)
+        for way, row, group in ((2, first - 1, UP), (3, last + 1, DOWN)):
+            for place, number in enumerate(group):
+                for plane in range(8):
+                    at = place * 8 + plane
+                    post[plane + 1, number, row : row + 1, :] = y_recv[step, way - 2, at : at + 1, :]
+        for way, number, plane, row, at in (
+            (4, 7, 0, first - 1, 7),
+            (5, 8, 9, last + 1, 0),
+            (6, 9, 0, last + 1, 0),
+            (7, 10, 9, first - 1, 7),
+        ):
+            post[plane, number, row : row + 1, :] = c_recv[step, way - 4, at : at + 1, :]
+
+    def work(step, plane, tile):
+        if step == 0:
+            f = [start[i, pl.ds(64 * tile + plane, 8, stride=8), :] for i in range(POPS)]
+        else:
+            f = [pull(posts.at[(step - 1) % 2], i, plane, tile) for i in range(POPS)]
+        post = collide(f, solid[plane, 8 * tile : 8 * tile + 8, :])
+        base = TOP + 8 * tile
+        for i in range(POPS):
+            posts[step % 2, plane + 1, i, base : base + 8, :] = post[i]
+
+    def inner(step):
+        def planes(plane, carry):
+            for tile in (1, 2):
+                work(step, plane, tile)
+            return carry
+
+        lax.fori_loop(1, 7, planes, 0)
+
+    def outer(step):
+        post = posts.at[step % 2]
+
+        def sides(side, carry):
+            for tile in range(4):
+                work(step, side * 7, tile)
+            return carry
+
+        lax.fori_loop(0, 2, sides, 0)
+        send_x(step, post)
+
+        def edges(plane, carry):
+            for tile in (0, 3):
+                work(step, plane, tile)
+            return carry
+
+        lax.fori_loop(1, 7, edges, 0)
+        send_y(step, post)
+
+    outer(0)
+    inner(0)
+    for step in range(1, STEPS):
+        inner(step)
+        receive(step - 1, posts.at[(step - 1) % 2])
+        outer(step)
+    post = posts.at[(STEPS - 1) % 2]
+
+    def finish(number):
+        def planes(plane, carry):
+            for tile in range(4):
+                result[number, pl.ds(64 * tile + plane, 8, stride=8), :] = pull(post, number, plane, tile)
+            return carry
+
+        lax.fori_loop(0, 8, planes, 0)
+        pltpu.make_async_copy(result.at[number], result_out.at[number], out_sem.at[number]).start()
+
+    for number in (0, 5, 6):
+        finish(number)
+    receive(STEPS - 1, post)
+    for number in range(POPS):
+        if number not in (0, 5, 6):
+            finish(number)
+    for step in range(STEPS):
+        for way in range(8):
+            copy(step, way).wait_send()
+    for number in range(POPS):
+        pltpu.make_async_copy(result.at[number], result_out.at[number], out_sem.at[number]).wait()
+
+
+def lattice_scratch():
+    return [
+        pltpu.VMEM((2, 10, POPS, TALL, LANES), jnp.float32),
+        pltpu.VMEM((STEPS, 2, 5 * ROWS, LANES), jnp.bfloat16),
+        pltpu.VMEM((STEPS, 2, 5 * ROWS, LANES), jnp.bfloat16),
+        pltpu.VMEM((STEPS, 2, 40, LANES), jnp.float32),
+        pltpu.VMEM((STEPS, 2, 40, LANES), jnp.float32),
+        pltpu.VMEM((STEPS, 4, 8, LANES), jnp.float32),
+        pltpu.VMEM((STEPS, 4, 8, LANES), jnp.float32),
+        pltpu.SemaphoreType.DMA((STEPS, 8)),
+        pltpu.SemaphoreType.DMA((STEPS, 8)),
+        pltpu.SemaphoreType.DMA((POPS,)),
+    ]
 
 
 def brick_slots(me, bricks, target_ref, count_ref, cell_ref, weight_ref, operand):
@@ -124,7 +292,7 @@
     node = lax.broadcasted_iota(jnp.int32, (blocks, nodes), 1).astype(jnp.float32)
     live = node < count_col
     cell = cell_ref[...]
-    high = ((cell >> 7) & 31) * 8 + (cell >> 12)
+    high = cell >> 7
     low = cell & 127
     weight = jnp.where(live, weight_ref[...].astype(jnp.float32), 0.0)
     for part in range(2):
@@ -202,11 +370,13 @@
     )
 
 
-def raster_kernel(
-    bricks, along_y, target_ref, count_ref, cell_ref, weight_ref, solid_ref,
-    operand, outgoing, arrived, total, sent_sem, arrived_sem,
+def program_kernel(
+    bricks, along_y, target_ref, count_ref, cell_ref, weight_ref, start_hbm, solid_ref, result_hbm,
+    operand, outgoing, arrived, total, start, solid, result, sent_sem, arrived_sem, start_sem, *lattice_refs,
 ):
     me = lax.axis_index("gx") * along_y + lax.axis_index("gy")
+    loading = pltpu.make_async_copy(start_hbm, start, start_sem)
+    loading.start()
     slot_row = brick_slots(me, bricks, target_ref, count_ref, cell_ref, weight_ref, operand)
     total[...] = jnp.zeros_like(total)
 
@@ -251,46 +421,61 @@
         return carry
 
     lax.fori_loop(0, bricks // GROUP, later, 0)
+    density = total[:, :LANES] + total[:, LANES:] * (1.0 / REST_SCALE)
+    fraction = density / (1.0 + density)
+    for plane in range(8):
+        for tile in range(4):
+            piece = fraction[plane * ROWS + 8 * tile : plane * ROWS + 8 * tile + 8, :]
+            solid[plane, 8 * tile : 8 * tile + 8, :] = piece
+            solid_ref[pl.ds(64 * tile + plane, 8, stride=8), :] = piece
+    loading.wait()
+    lattice(start, solid, result, result_hbm, *lattice_refs)
     everything = outgoing.at[pl.ds(1, bricks - 1)]
     pltpu.make_async_copy(everything, everything, sent_sem).wait()
-    density = total[:, :LANES] + total[:, LANES:] * (1.0 / REST_SCALE)
-    solid_ref[...] = density / (1.0 + density)
-
-
-def rasterize(block_brick, node_count, node_cell, node_weight, bricks, along_y):
+
+
+def to_rows(values):
+    lead = values.shape[:-2]
+    return jnp.swapaxes(values.reshape(lead + (8, ROWS, LANES)), -3, -2).reshape(lead + (8 * ROWS, LANES))
+
+
+def from_rows(values):
+    lead = values.shape[:-2]
+    return jnp.swapaxes(values.reshape(lead + (ROWS, 8, LANES)), -3, -2).reshape(lead + (8, ROWS * LANES))
+
+
+def on_device(populations, node_cell, node_weight, node_count, block_brick):
+    along_y = lax.axis_size("gy")
+    bricks = lax.axis_size("gx") * along_y
     blocks, nodes = node_cell.shape
-    return pl.pallas_call(
-        functools.partial(raster_kernel, bricks, along_y),
-        out_shape=jax.ShapeDtypeStruct((256, LANES), jnp.float32),
-        in_specs=[pl.BlockSpec(memory_space=pltpu.VMEM)] * 4,
-        out_specs=pl.BlockSpec(memory_space=pltpu.VMEM),
+    vmem, anywhere = pl.BlockSpec(memory_space=pltpu.VMEM), pl.BlockSpec(memory_space=pl.ANY)
+    solid, result = pl.pallas_call(
+        functools.partial(program_kernel, bricks, along_y),
+        out_shape=(
+            jax.ShapeDtypeStruct((8 * ROWS, LANES), jnp.float32),
+            jax.ShapeDtypeStruct((POPS, 8 * ROWS, LANES), jnp.float32),
+        ),
+        in_specs=[vmem, vmem, vmem, vmem, anywhere],
+        out_specs=(vmem, anywhere),
         scratch_shapes=[
             pltpu.VMEM((blocks, 6 * LANES), jnp.bfloat16),
             pltpu.VMEM((bricks, 8, LANES), jnp.int32),
             pltpu.VMEM((bricks, 8, LANES), jnp.int32),
-            pltpu.VMEM((256, 2 * LANES), jnp.float32),
+            pltpu.VMEM((8 * ROWS, 2 * LANES), jnp.float32),
+            pltpu.VMEM((POPS, 8 * ROWS, LANES), jnp.float32),
+            pltpu.VMEM((8, ROWS, LANES), jnp.float32),
+            pltpu.VMEM((POPS, 8 * ROWS, LANES), jnp.float32),
             pltpu.SemaphoreType.DMA,
             pltpu.SemaphoreType.DMA((bricks // GROUP,)),
-        ],
+            pltpu.SemaphoreType.DMA,
+        ]
+        + lattice_scratch(),
         compiler_params=pltpu.CompilerParams(
             has_side_effects=True, vmem_limit_bytes=48 * 1024 * 1024
         ),
-        name="rasterize",
-    )(block_brick, node_count.reshape(1, blocks), node_cell, node_weight)
-
-
-def on_device(populations, node_cell, node_weight, node_count, block_brick):
-    along_y = lax.axis_size("gy")
-    bricks = lax.axis_size("gx") * along_y
-    solid = rasterize(block_brick, node_count, node_cell, node_weight, bricks, along_y)
-    solid_frac = solid.reshape(32, 8, LANES).transpose(1, 0, 2).reshape(8, 32 * LANES)
-    current = populations
-    for repeat in range(STEPS):
-        collided = collide(current, solid_frac)
-        padded = extended(collided, (("gx", 1),), 1)
-        padded = extended(padded, (("gy", 2),), NZ)
-        current = stream_pull(padded)
-    return (current, solid_frac)
+        name="permeability",
+    )(block_brick, node_count.reshape(1, blocks), node_cell, node_weight, to_rows(populations))
+    return (from_rows(result), from_rows(solid))
 
 
 def solution(mesh):

time: 159 us -> 72.3 us (0.45)
  other arithmetic: 35.8 us -> 0 us
  waiting for transfers between devices: 35 us -> 0 us
  Pallas kernels: 35.7 us -> 64.2 us
  starting transfers between devices: 23.8 us -> 0 us
  local copies, waits for them, and re-layouts: 25.6 us -> 7.22 us
  between operations: 2.67 us -> 0.66 us
    ppermute x12 -> x0, waiting for transfers between devices: 35 us -> none  [the longest x6 21.9 us: extended(): lax.ppermute(lax.slice_in_dim(block, block.shape[dim] - width, None, axis...]
    pallas_call x1, Pallas kernels: 35.7 us -> 64.2 us  [on_device(): pl.pallas_call(functools.partial(program_kernel, bricks, along_y), out_sh...]
    ppermute x12 -> x0, starting transfers between devices: 23.8 us -> none  [the longest x6 18.7 us: extended(): lax.ppermute(lax.slice_in_dim(block, 0, width, axis=dim), axis, backward)]
    unnamed x44 -> x0, other arithmetic: 12.4 us -> none
    gather x3 -> x0, local copies, waits for them, and re-layouts: 11.9 us -> none  [collide(): reversed_pops = incoming[np.array(opposite_of)]]
    mul x5 -> x0, other arithmetic: 7.3 us -> none  [the longest x4 7.23 us: collide(): projected = x_dir * velocity_x + y_dir * velocity_y + z_dir * velocity_z]
    add x3 -> x0, other arithmetic: 7.01 us -> none  [collide(): (1.0 - solid) * (incoming + relax_rate * (equilibrium - incoming))]
    concatenate x120 -> x0, local copies, waits for them, and re-layouts: 5.25 us -> none  [the longest x60 2.63 us: roll_within(): shifted = jnp.roll(values, offset, axis=-1)]
  transfers between devices with their start and end apart: 12 -> 0, of which waited for: 9 -> 0; matrix products, arithmetic and copies ran while one was open for 3% -> 0% of each run, Pallas kernels for 0% -> 0%
where the time goes in v2:
time: 72.3 us; the launch traced here: 72.1 us
  Pallas kernels  64.2 us (89%)
  local copies, waits for them, and re-layouts  7.22 us (10%)
    pallas_call x1, Pallas kernels, on_device(): pl.pallas_call(functools.partial(program_kernel, bricks, along_y), out_sh...  64.2 us
    unnamed x9, local copies, waits for them, and re-layouts  6.54 us

profile of v2, /device:TPU:1, one launch (start us, length us, event | category | flops | bytes accessed | tf_op | source)
XLA Modules:
  0.0 72.1 jit_solution(9013432615535327610)
XLA Ops:
  0.6 0.7 reshape.25.count_ref
  1.3 0.8 %copy.7.target_ref = s32[384,1]{1,0:T(8,128)S(1)} copy(s32[384,1]{0,1:T(1,128)} %param.9) | data formatting | bytes 3072 | tf_op args[4]
  2.1 0.0 copy-start
  2.1 1.7 %copy-done = f32[19,8,4096]{2,1,0:T(8,128)S(1)} copy-done((f32[19,8,4096]{2,1,0:T(8,128)S(1)}, f32[19,8,4096]{2,1,0:T(8,128)}, u32[]{:S(2)}) %copy-start) | copy-done | bytes 2490392
  3.8 0.0 copy-start.1
  3.8 1.0 %copy-done.1 = s32[384,256]{1,0:T(8,128)S(1)} copy-done((s32[384,256]{1,0:T(8,128)S(1)}, s32[384,256]{1,0:T(8,128)}, u32[]{:S(2)}) %copy-start.1) | copy-done | bytes 393240
  4.8 0.0 copy-start.2
  4.8 0.9 %copy-done.2 = bf16[384,256]{1,0:T(8,128)(2,1)S(1)} copy-done((bf16[384,256]{1,0:T(8,128)(2,1)S(1)}, bf16[384,256]{1,0:T(8,128)(2,1)}, u32[]{:S(2)}) %copy-start.2) | copy-done | bytes 196632
  5.8 64.2 %permeability.1 = (f32[256,128]{1,0:T(8,128)S(1)}, f32[19,256,128]{2,1,0:T(8,128)S(1)}) custom-call(s32[384,1]{1,0:T(8,128)S(1)} %copy.7.target_ref, s32[1,384]{1,0:T(1,128)S(1)} %reshape.25.count_ref, s32[384,256]{1,0:T(8,128)S(1)} %copy-done.1, bf16[384,256]{1,0:T(8,128)(2,1)S(1)} %copy-done.2, f32[19,256,128]{2,1,0:T(8,128)S(1)} %bitcast.15), custom_call_target="tpu_custom_call" | custom-call | tf_op jit(solution)/shard_map/permeability/pallas_call | solution.py:452
  70.0 1.5 %copy.10 = f32[19,8,4096]{2,1,0:T(8,128)} copy(f32[19,8,4096]{2,1,0:T(8,128)S(1)} %bitcast.16) | data formatting | bytes 4980736
  71.4 0.7 copy.11
Async XLA Ops:
  2.1 1.7 %copy-start = (f32[19,8,4096]{2,1,0:T(8,128)S(1)}, f32[19,8,4096]{2,1,0:T(8,128)}, u32[]{:S(2)}) copy-start(f32[19,8,4096]{2,1,0:T(8,128)} %param.5) | copy-start | bytes 7471108
  3.8 1.0 %copy-start.1 = (s32[384,256]{1,0:T(8,128)S(1)}, s32[384,256]{1,0:T(8,128)}, u32[]{:S(2)}) copy-start(s32[384,256]{1,0:T(8,128)} %cell_ref.1) | copy-start | bytes 1179652
  4.8 0.9 %copy-start.2 = (bf16[384,256]{1,0:T(8,128)(2,1)S(1)}, bf16[384,256]{1,0:T(8,128)(2,1)}, u32[]{:S(2)}) copy-start(bf16[384,256]{1,0:T(8,128)(2,1)} %weight_ref.1) | copy-start | bytes 589828

commit v3 on v2

--- a/solution.py
+++ b/solution.py
@@ -53,6 +53,7 @@
 LEFT = (2, 8, 10, 12, 14)
 UP = (3, 7, 10, 15, 17)
 DOWN = (4, 8, 9, 16, 18)
+UNSHIFTED = (0, 5, 6)
 
 
 def place_of_lane():
@@ -118,7 +119,7 @@
     return post
 
 
-def lattice(start, solid, result, result_out, posts, x_send, x_recv, y_send, y_recv, c_send, c_recv, sent, came, out_sem):
+def lattice(start, solid, result, posts, x_send, x_recv, y_send, y_recv, c_send, c_recv, sent, came):
     here_x, here_y = lax.axis_index("gx"), lax.axis_index("gy")
     along_x, along_y = lax.axis_size("gx"), lax.axis_size("gy")
     ahead_x, behind_x = lax.rem(here_x + 1, along_x), lax.rem(here_x + along_x - 1, along_x)
@@ -238,26 +239,21 @@
         outer(step)
     post = posts.at[(STEPS - 1) % 2]
 
-    def finish(number):
+    def finish(numbers):
         def planes(plane, carry):
-            for tile in range(4):
-                result[number, pl.ds(64 * tile + plane, 8, stride=8), :] = pull(post, number, plane, tile)
+            for number in numbers:
+                for tile in range(4):
+                    result[number, pl.ds(64 * tile + plane, 8, stride=8), :] = pull(post, number, plane, tile)
             return carry
 
         lax.fori_loop(0, 8, planes, 0)
-        pltpu.make_async_copy(result.at[number], result_out.at[number], out_sem.at[number]).start()
-
-    for number in (0, 5, 6):
-        finish(number)
+
+    finish(UNSHIFTED)
     receive(STEPS - 1, post)
-    for number in range(POPS):
-        if number not in (0, 5, 6):
-            finish(number)
+    finish([number for number in range(POPS) if number not in UNSHIFTED])
     for step in range(STEPS):
         for way in range(8):
             copy(step, way).wait_send()
-    for number in range(POPS):
-        pltpu.make_async_copy(result.at[number], result_out.at[number], out_sem.at[number]).wait()
 
 
 def lattice_scratch():
@@ -271,7 +267,6 @@
         pltpu.VMEM((STEPS, 4, 8, LANES), jnp.float32),
         pltpu.SemaphoreType.DMA((STEPS, 8)),
         pltpu.SemaphoreType.DMA((STEPS, 8)),
-        pltpu.SemaphoreType.DMA((POPS,)),
     ]
 
 
@@ -279,15 +274,16 @@
     blocks, nodes = cell_ref.shape
     row = lax.broadcasted_iota(jnp.int32, (blocks, blocks), 0)
     col = lax.broadcasted_iota(jnp.int32, (blocks, blocks), 1)
-    target_col = target_ref[...]
+    target_row = target_ref[...].astype(jnp.float32)
+    target_col = jnp.sum(jnp.where(row == col, target_row, 0.0), axis=1, keepdims=True)
     brick = lax.broadcasted_iota(jnp.int32, (blocks, bricks), 1)
-    matches = jnp.where(brick == target_col, 1.0, 0.0)
+    matches = jnp.where(brick.astype(jnp.float32) == target_col, 1.0, 0.0)
     before = jnp.where(col < row, 1.0, 0.0).astype(jnp.bfloat16)
     earlier = jnp.dot(before, matches.astype(jnp.bfloat16), preferred_element_type=jnp.float32)
     rank = jnp.sum(earlier * matches, axis=1, keepdims=True)
-    slot_col = target_col.astype(jnp.float32) * CAP + rank
+    slot_col = target_col * CAP + rank
     slot_row = jnp.sum(jnp.where(row == col, slot_col, 0.0), axis=0, keepdims=True)
-    count_row = count_ref[...].astype(jnp.float32)
+    count_row = count_ref[...].astype(jnp.float32).reshape(1, blocks)
     count_col = jnp.sum(jnp.where(row == col, count_row, 0.0), axis=1, keepdims=True)
     node = lax.broadcasted_iota(jnp.int32, (blocks, nodes), 1).astype(jnp.float32)
     live = node < count_col
@@ -371,13 +367,33 @@
 
 
 def program_kernel(
-    bricks, along_y, target_ref, count_ref, cell_ref, weight_ref, start_hbm, solid_ref, result_hbm,
-    operand, outgoing, arrived, total, start, solid, result, sent_sem, arrived_sem, start_sem, *lattice_refs,
+    bricks, along_y, target_hbm, count_hbm, cell_hbm, weight_hbm, start_hbm, solid_ref, result,
+    target_ref, count_ref, cell_ref, weight_ref, start, operand, outgoing, arrived, total, solid,
+    load_sem, sent_sem, arrived_sem, *lattice_refs,
 ):
     me = lax.axis_index("gx") * along_y + lax.axis_index("gy")
-    loading = pltpu.make_async_copy(start_hbm, start, start_sem)
-    loading.start()
+    sources = (target_hbm, count_hbm, cell_hbm, weight_hbm, start_hbm)
+    landings = (target_ref, count_ref, cell_ref, weight_ref, start)
+    loads = [
+        pltpu.make_async_copy(source, landing, load_sem.at[number])
+        for number, (source, landing) in enumerate(zip(sources, landings))
+    ]
+    for load in loads:
+        load.start()
+    barrier = pltpu.get_barrier_semaphore()
+
+    def greet(step, carry):
+        target = lax.rem(me + step, bricks)
+        pl.semaphore_signal(
+            barrier, inc=1, device_id=(target // along_y, lax.rem(target, along_y)), device_id_type=MESH
+        )
+        return carry
+
+    lax.fori_loop(1, bricks, greet, 0)
+    for load in loads[:4]:
+        load.wait()
     slot_row = brick_slots(me, bricks, target_ref, count_ref, cell_ref, weight_ref, operand)
+    pl.semaphore_wait(barrier, bricks - 1)
     total[...] = jnp.zeros_like(total)
 
     def send(chunk, carry):
@@ -428,8 +444,8 @@
             piece = fraction[plane * ROWS + 8 * tile : plane * ROWS + 8 * tile + 8, :]
             solid[plane, 8 * tile : 8 * tile + 8, :] = piece
             solid_ref[pl.ds(64 * tile + plane, 8, stride=8), :] = piece
-    loading.wait()
-    lattice(start, solid, result, result_hbm, *lattice_refs)
+    loads[4].wait()
+    lattice(start, solid, result, *lattice_refs)
     everything = outgoing.at[pl.ds(1, bricks - 1)]
     pltpu.make_async_copy(everything, everything, sent_sem).wait()
 
@@ -448,33 +464,43 @@
     along_y = lax.axis_size("gy")
     bricks = lax.axis_size("gx") * along_y
     blocks, nodes = node_cell.shape
-    vmem, anywhere = pl.BlockSpec(memory_space=pltpu.VMEM), pl.BlockSpec(memory_space=pl.ANY)
+    vmem, hbm = pl.BlockSpec(memory_space=pltpu.VMEM), pl.BlockSpec(memory_space=pltpu.HBM)
     solid, result = pl.pallas_call(
         functools.partial(program_kernel, bricks, along_y),
         out_shape=(
             jax.ShapeDtypeStruct((8 * ROWS, LANES), jnp.float32),
             jax.ShapeDtypeStruct((POPS, 8 * ROWS, LANES), jnp.float32),
         ),
-        in_specs=[vmem, vmem, vmem, vmem, anywhere],
-        out_specs=(vmem, anywhere),
+        in_specs=[hbm] * 5,
+        out_specs=(vmem, vmem),
         scratch_shapes=[
+            pltpu.VMEM((1, blocks), jnp.int32),
+            pltpu.VMEM((blocks,), jnp.int32),
+            pltpu.VMEM((blocks, nodes), jnp.int32),
+            pltpu.VMEM((blocks, nodes), jnp.bfloat16),
+            pltpu.VMEM((POPS, 8 * ROWS, LANES), jnp.float32),
             pltpu.VMEM((blocks, 6 * LANES), jnp.bfloat16),
             pltpu.VMEM((bricks, 8, LANES), jnp.int32),
             pltpu.VMEM((bricks, 8, LANES), jnp.int32),
             pltpu.VMEM((8 * ROWS, 2 * LANES), jnp.float32),
-            pltpu.VMEM((POPS, 8 * ROWS, LANES), jnp.float32),
             pltpu.VMEM((8, ROWS, LANES), jnp.float32),
-            pltpu.VMEM((POPS, 8 * ROWS, LANES), jnp.float32),
+            pltpu.SemaphoreType.DMA((5,)),
             pltpu.SemaphoreType.DMA,
             pltpu.SemaphoreType.DMA((bricks // GROUP,)),
-            pltpu.SemaphoreType.DMA,
         ]
         + lattice_scratch(),
         compiler_params=pltpu.CompilerParams(
-            has_side_effects=True, vmem_limit_bytes=48 * 1024 * 1024
+            collective_id=0, has_side_effects=True, vmem_limit_bytes=48 * 1024 * 1024
         ),
         name="permeability",
-    )(block_brick, node_count.reshape(1, blocks), node_cell, node_weight, to_rows(populations))
+    )(
+        *(
+            pltpu.with_memory_space_constraint(operand, pltpu.HBM)
+            for operand in (
+                block_brick.reshape(1, blocks), node_count, node_cell, node_weight, to_rows(populations)
+            )
+        )
+    )
     return (from_rows(result), from_rows(solid))
 
 

time: 72.3 us -> 52.6 us (0.73)
  Pallas kernels: 64.2 us -> 49.7 us
  local copies, waits for them, and re-layouts: 7.22 us -> 2.11 us
    pallas_call x1, Pallas kernels: 64.2 us -> 49.7 us  [on_device(): pl.pallas_call(functools.partial(program_kernel, bricks, along_y), out_sh...]
    unnamed x9 -> x2, local copies, waits for them, and re-layouts: 6.54 us -> 2.11 us
where the time goes in v3:
time: 52.6 us; the launch traced here: 52.5 us
  Pallas kernels  49.7 us (94%)
  local copies, waits for them, and re-layouts  2.11 us (4%)
  between operations  0.64 us (1%)
    pallas_call x1, Pallas kernels, on_device(): pl.pallas_call(functools.partial(program_kernel, bricks, along_y), out_sh...  49.7 us
    unnamed x2, local copies, waits for them, and re-layouts  2.11 us

profile of v3, /device:TPU:1, one launch (start us, length us, event | category | flops | bytes accessed | tf_op | source)
XLA Modules:
  0.0 52.5 jit_solution(5966693109204032854)
XLA Ops:
  0.6 49.7 %permeability.1 = (f32[256,128]{1,0:T(8,128)S(1)}, f32[19,256,128]{2,1,0:T(8,128)S(1)}) custom-call(s32[1,384]{1,0:T(1,128)} %bitcast.19, s32[384]{0:T(512)} %count_hbm.1, s32[384,256]{1,0:T(8,128)} %cell_hbm.1, bf16[384,256]{1,0:T(8,128)(2,1)} %weight_hbm.1, f32[19,256,128]{2,1,0:T(8,128)} %bitcast.18), custom_call_target="tpu_custom_call" | custom-call | tf_op jit(solution)/shard_map/permeability/pallas_call | solution.py:468
  50.4 1.5 %copy.9 = f32[19,8,4096]{2,1,0:T(8,128)} copy(f32[19,8,4096]{2,1,0:T(8,128)S(1)} %bitcast.16) | data formatting | bytes 4980736
  51.8 0.7 %copy.10 = f32[8,4096]{1,0:T(8,128)} copy(f32[8,4096]{1,0:T(8,128)S(1)} %bitcast.17) | data formatting | bytes 262144

commit v4 on v3

--- a/solution.py
+++ b/solution.py
@@ -12,7 +12,7 @@
 STEPS = 3
 CAP = 4
 LANES = 128
-GROUP = 8
+GROUP = 16
 CHUNK = 16
 WEIGHT_STEPS = 1024.0
 REST_SCALE = 64.0
@@ -53,31 +53,40 @@
 LEFT = (2, 8, 10, 12, 14)
 UP = (3, 7, 10, 15, 17)
 DOWN = (4, 8, 9, 16, 18)
-UNSHIFTED = (0, 5, 6)
-
-
-def place_of_lane():
-    lane = lax.broadcasted_iota(jnp.int32, (8, LANES), 1)
-    return lane < NZ, (lane & (NZ - 1)) == 0, (lane & (NZ - 1)) == NZ - 1
+UNSHIFTED = (0, 5)
 
 
 def pull(post, number, plane, tile):
     shift_x, shift_y, shift_z = lattice_velocities[number]
-    even, z_first, z_last = place_of_lane()
+    even = lax.broadcasted_iota(jnp.int32, (8, LANES), 1) < NZ
     base = TOP + 8 * tile
     values = post[plane + 1 - shift_x, number, base : base + 8, :]
-    turn = 0
+    turn = shift_z
     if shift_y == 1:
         values = jnp.where(even, values, post[plane + 1 - shift_x, number, base - 1 : base + 7, :])
-        turn = NZ
+        turn += NZ
     if shift_y == -1:
         values = jnp.where(even, post[plane + 1 - shift_x, number, base + 1 : base + 9, :], values)
-        turn = NZ
+        turn += NZ
+    return pltpu.roll(values, turn % LANES, 1) if turn else values
+
+
+def pull_pair(post, number, plane, tile):
+    pair = [pull(post, number, plane, tile), pull(post, number + 1, plane, tile)]
+    shift_z = lattice_velocities[number][2]
     if shift_z == 0:
-        return pltpu.roll(values, turn, 1) if turn else values
-    near = pltpu.roll(values, (shift_z + turn) % LANES, 1)
-    wrapped = pltpu.roll(values, (shift_z - shift_z * NZ + turn) % LANES, 1)
-    return jnp.where(z_first if shift_z == 1 else z_last, wrapped, near)
+        return pair
+    z_place = lax.broadcasted_iota(jnp.int32, (8, LANES), 1) & (NZ - 1)
+    edge, other = (0, NZ - 1) if shift_z == 1 else (NZ - 1, 0)
+    turned = pltpu.roll(jnp.where(z_place == edge, pair[0], pair[1]), NZ, 1)
+    return [jnp.where(z_place == edge, turned, pair[0]), jnp.where(z_place == other, turned, pair[1])]
+
+
+def pull_all(post, plane, tile):
+    values = [pull(post, 0, plane, tile)]
+    for number in range(1, POPS, 2):
+        values += pull_pair(post, number, plane, tile)
+    return values
 
 
 def collide(f, solid):
@@ -198,7 +207,7 @@
         if step == 0:
             f = [start[i, pl.ds(64 * tile + plane, 8, stride=8), :] for i in range(POPS)]
         else:
-            f = [pull(posts.at[(step - 1) % 2], i, plane, tile) for i in range(POPS)]
+            f = pull_all(posts.at[(step - 1) % 2], plane, tile)
         post = collide(f, solid[plane, 8 * tile : 8 * tile + 8, :])
         base = TOP + 8 * tile
         for i in range(POPS):
@@ -241,16 +250,20 @@
 
     def finish(numbers):
         def planes(plane, carry):
-            for number in numbers:
-                for tile in range(4):
-                    result[number, pl.ds(64 * tile + plane, 8, stride=8), :] = pull(post, number, plane, tile)
+            for tile in range(4):
+                at = pl.ds(64 * tile + plane, 8, stride=8)
+                for number in numbers:
+                    if number == 0:
+                        result[0, at, :] = pull(post, 0, plane, tile)
+                    else:
+                        result[number, at, :], result[number + 1, at, :] = pull_pair(post, number, plane, tile)
             return carry
 
         lax.fori_loop(0, 8, planes, 0)
 
     finish(UNSHIFTED)
     receive(STEPS - 1, post)
-    finish([number for number in range(POPS) if number not in UNSHIFTED])
+    finish([number for number in range(1, POPS, 2) if number not in UNSHIFTED])
     for step in range(STEPS):
         for way in range(8):
             copy(step, way).wait_send()
@@ -299,44 +312,35 @@
     return slot_row
 
 
-def send_chunk(me, bricks, along_y, chunk, slot_row, operand, outgoing, arrived, sent_sem, arrived_sem):
+def gather_slots(me, bricks, slot_row, operand, outgoing):
     rows = CHUNK * 8
     place = lax.broadcasted_iota(jnp.int32, (rows, 1), 0)
-    offset = chunk * CHUNK + (place >> 3)
-    wanted = lax.rem(me + offset, bricks) * CAP + (place & (CAP - 1))
-    pick = jnp.where(wanted.astype(jnp.float32) == slot_row, 1.0, 0.0).astype(jnp.bfloat16)
-    found = jnp.dot(pick, operand[...], preferred_element_type=jnp.float32)
-    lower = (place & 7) < CAP
-    high, low, weight = [
-        jnp.where(
-            lower,
-            found[:, number * LANES : (number + 1) * LANES],
-            found[:, (3 + number) * LANES : (4 + number) * LANES],
-        )
-        for number in range(3)
-    ]
-    packed = ((weight * WEIGHT_STEPS).astype(jnp.int32) << 15) + (high * LANES + low).astype(jnp.int32)
-    base = pl.multiple_of(chunk * CHUNK, CHUNK)
-    outgoing[pl.ds(base, CHUNK)] = packed.reshape(CHUNK, 8, LANES)
-
-    def start(place_in, carry):
-        step = base + place_in
-        target = lax.rem(me + step, bricks)
-
-        @pl.when(step > 0)
-        def _():
-            pltpu.make_async_remote_copy(
-                src_ref=outgoing.at[step],
-                dst_ref=arrived.at[step],
-                send_sem=sent_sem,
-                recv_sem=arrived_sem.at[step // GROUP],
-                device_id=(target // along_y, lax.rem(target, along_y)),
-                device_id_type=MESH,
-            ).start()
-
+
+    def chunk_of(chunk, carry):
+        offset = chunk * CHUNK + (place >> 3)
+        wanted = lax.rem(me + offset, bricks) * CAP + (place & (CAP - 1))
+        pick = jnp.where(wanted.astype(jnp.float32) == slot_row, 1.0, 0.0).astype(jnp.bfloat16)
+        found = jnp.dot(pick, operand[...], preferred_element_type=jnp.float32)
+        lower = (place & 7) < CAP
+        high, low, weight = [
+            jnp.where(
+                lower,
+                found[:, number * LANES : (number + 1) * LANES],
+                found[:, (3 + number) * LANES : (4 + number) * LANES],
+            )
+            for number in range(3)
+        ]
+        packed = ((weight * WEIGHT_STEPS).astype(jnp.int32) << 15) + (high * LANES + low).astype(jnp.int32)
+        base = pl.multiple_of(chunk * CHUNK, CHUNK)
+        outgoing[pl.ds(base, CHUNK)] = packed.reshape(CHUNK, 8, LANES)
         return carry
 
-    lax.fori_loop(0, CHUNK, start, 0)
+    lax.fori_loop(0, bricks // CHUNK, chunk_of, 0)
+
+
+def device_at(me, step, bricks, along_y):
+    target = lax.rem(me + step, bricks)
+    return lax.div(target, along_y), lax.rem(target, along_y)
 
 
 def one_hots(values, line):
@@ -383,9 +387,8 @@
     barrier = pltpu.get_barrier_semaphore()
 
     def greet(step, carry):
-        target = lax.rem(me + step, bricks)
         pl.semaphore_signal(
-            barrier, inc=1, device_id=(target // along_y, lax.rem(target, along_y)), device_id_type=MESH
+            barrier, inc=1, device_id=device_at(me, step, bricks, along_y), device_id_type=MESH
         )
         return carry
 
@@ -393,16 +396,22 @@
     for load in loads[:4]:
         load.wait()
     slot_row = brick_slots(me, bricks, target_ref, count_ref, cell_ref, weight_ref, operand)
+    gather_slots(me, bricks, slot_row, operand, outgoing)
+    total[...] = jnp.zeros_like(total)
     pl.semaphore_wait(barrier, bricks - 1)
-    total[...] = jnp.zeros_like(total)
-
-    def send(chunk, carry):
-        send_chunk(
-            me, bricks, along_y, chunk, slot_row, operand, outgoing, arrived, sent_sem, arrived_sem
-        )
+
+    def send(step, carry):
+        pltpu.make_async_remote_copy(
+            src_ref=outgoing.at[step],
+            dst_ref=arrived.at[step],
+            send_sem=sent_sem,
+            recv_sem=arrived_sem.at[lax.div(step, GROUP)],
+            device_id=device_at(me, step, bricks, along_y),
+            device_id_type=MESH,
+        ).start()
         return carry
 
-    lax.fori_loop(0, bricks // CHUNK, send, 0)
+    lax.fori_loop(1, bricks, send, 0)
     arrived[0] = outgoing[0]
 
     def add(group):

time: 52.6 us -> 51.5 us (0.979)
  Pallas kernels: 49.7 us -> 48.6 us
    pallas_call x1, Pallas kernels: 49.7 us -> 48.6 us  [on_device(): pl.pallas_call(functools.partial(program_kernel, bricks, along_y), out_sh...]
where the time goes in v4:
time: 51.5 us; the launch traced here: 51.4 us
  Pallas kernels  48.6 us (94%)
  local copies, waits for them, and re-layouts  2.11 us (4%)
  between operations  0.64 us (1%)
    pallas_call x1, Pallas kernels, on_device(): pl.pallas_call(functools.partial(program_kernel, bricks, along_y), out_sh...  48.6 us
    unnamed x2, local copies, waits for them, and re-layouts  2.11 us

profile of v4, /device:TPU:1, one launch (start us, length us, event | category | flops | bytes accessed | tf_op | source)
XLA Modules:
  0.0 51.4 jit_solution(14216809044492146061)
XLA Ops:
  0.6 48.6 %permeability.1 = (f32[256,128]{1,0:T(8,128)S(1)}, f32[19,256,128]{2,1,0:T(8,128)S(1)}) custom-call(s32[1,384]{1,0:T(1,128)} %bitcast.19, s32[384]{0:T(512)} %count_hbm.1, s32[384,256]{1,0:T(8,128)} %cell_hbm.1, bf16[384,256]{1,0:T(8,128)(2,1)} %weight_hbm.1, f32[19,256,128]{2,1,0:T(8,128)} %bitcast.18), custom_call_target="tpu_custom_call" | custom-call | tf_op jit(solution)/shard_map/permeability/pallas_call | solution.py:477
  49.3 1.5 %copy.9 = f32[19,8,4096]{2,1,0:T(8,128)} copy(f32[19,8,4096]{2,1,0:T(8,128)S(1)} %bitcast.16) | data formatting | bytes 4980736
  50.7 0.7 %copy.10 = f32[8,4096]{1,0:T(8,128)} copy(f32[8,4096]{1,0:T(8,128)S(1)} %bitcast.17) | data formatting | bytes 262144

commit v5 on v4

--- a/solution.py
+++ b/solution.py
@@ -49,30 +49,26 @@
 TOP = 8
 TALL = 48
 POPS = 19
-RIGHT = (1, 7, 9, 11, 13)
-LEFT = (2, 8, 10, 12, 14)
-UP = (3, 7, 10, 15, 17)
-DOWN = (4, 8, 9, 16, 18)
-UNSHIFTED = (0, 5)
-
-
-def pull(post, number, plane, tile):
+WIDE = STEPS
+PLANES = 8 + 2 * WIDE
+
+
+def pull(read, number):
     shift_x, shift_y, shift_z = lattice_velocities[number]
     even = lax.broadcasted_iota(jnp.int32, (8, LANES), 1) < NZ
-    base = TOP + 8 * tile
-    values = post[plane + 1 - shift_x, number, base : base + 8, :]
+    values = read(number, shift_x, 0)
     turn = shift_z
     if shift_y == 1:
-        values = jnp.where(even, values, post[plane + 1 - shift_x, number, base - 1 : base + 7, :])
+        values = jnp.where(even, values, read(number, shift_x, -1))
         turn += NZ
     if shift_y == -1:
-        values = jnp.where(even, post[plane + 1 - shift_x, number, base + 1 : base + 9, :], values)
+        values = jnp.where(even, read(number, shift_x, 1), values)
         turn += NZ
     return pltpu.roll(values, turn % LANES, 1) if turn else values
 
 
-def pull_pair(post, number, plane, tile):
-    pair = [pull(post, number, plane, tile), pull(post, number + 1, plane, tile)]
+def pull_pair(read, number):
+    pair = [pull(read, number), pull(read, number + 1)]
     shift_z = lattice_velocities[number][2]
     if shift_z == 0:
         return pair
@@ -82,10 +78,10 @@
     return [jnp.where(z_place == edge, turned, pair[0]), jnp.where(z_place == other, turned, pair[1])]
 
 
-def pull_all(post, plane, tile):
-    values = [pull(post, 0, plane, tile)]
+def pull_all(read):
+    values = [pull(read, 0)]
     for number in range(1, POPS, 2):
-        values += pull_pair(post, number, plane, tile)
+        values += pull_pair(read, number)
     return values
 
 
@@ -128,12 +124,12 @@
     return post
 
 
-def lattice(start, solid, result, posts, x_send, x_recv, y_send, y_recv, c_send, c_recv, sent, came):
+def partner_devices():
     here_x, here_y = lax.axis_index("gx"), lax.axis_index("gy")
     along_x, along_y = lax.axis_size("gx"), lax.axis_size("gy")
     ahead_x, behind_x = lax.rem(here_x + 1, along_x), lax.rem(here_x + along_x - 1, along_x)
     ahead_y, behind_y = lax.rem(here_y + 1, along_y), lax.rem(here_y + along_y - 1, along_y)
-    partners = (
+    return (
         (ahead_x, here_y),
         (behind_x, here_y),
         (here_x, ahead_y),
@@ -143,143 +139,185 @@
         (ahead_x, behind_y),
         (behind_x, ahead_y),
     )
-    first, last = TOP, TOP + ROWS - 1
-
-    def copy(step, way):
-        if way < 2:
-            source, landing = x_send.at[step, way], x_recv.at[step, way]
-        elif way < 4:
-            source, landing = y_send.at[step, way - 2], y_recv.at[step, way - 2]
-        else:
-            source, landing = c_send.at[step, way - 4], c_recv.at[step, way - 4]
-        return pltpu.make_async_remote_copy(
-            src_ref=source,
-            dst_ref=landing,
-            send_sem=sent.at[step, way],
-            recv_sem=came.at[step, way],
-            device_id=partners[way],
-            device_id_type=MESH,
-        )
-
-    def send_x(step, post):
-        for way, plane, group in ((0, 8, RIGHT), (1, 1, LEFT)):
-            for place, number in enumerate(group):
+
+
+SIDE = {2: 0, 4: 0, 7: 0, 3: 1, 5: 1, 6: 1}
+HALO_WAYS = ((2, 4, 7), (3, 6, 5))
+
+
+def start_copy(way, partners, x_send, x_recv, y_send, y_recv, sent, came):
+    if way < 2:
+        source, landing = x_send.at[way], x_recv.at[way]
+    else:
+        source, landing = y_send.at[SIDE[way]], y_recv.at[way - 2]
+    return pltpu.make_async_remote_copy(
+        src_ref=source, dst_ref=landing, send_sem=sent.at[way], recv_sem=came.at[way],
+        device_id=partners[way], device_id_type=MESH,
+    )
+
+
+def solid_copy(way, partners, solid, y_send, y_recv, sent, came):
+    if way == 0:
+        source, landing = solid.at[pl.ds(8, WIDE)], solid.at[pl.ds(0, WIDE)]
+    elif way == 1:
+        source, landing = solid.at[pl.ds(WIDE, WIDE)], solid.at[pl.ds(8 + WIDE, WIDE)]
+    else:
+        source, landing = y_send.at[SIDE[way]], y_recv.at[way - 2]
+    return pltpu.make_async_remote_copy(
+        src_ref=source, dst_ref=landing, send_sem=sent.at[way], recv_sem=came.at[way],
+        device_id=partners[way], device_id_type=MESH,
+    )
+
+
+def pack_start(start, x_send, y_send):
+    def population(number, carry):
+        for way, first in ((0, 8 - WIDE), (1, 0)):
+            for plane in range(WIDE):
                 for half in range(2):
-                    values = post[plane, number, first + 16 * half : first + 16 * half + 16, :]
-                    at = place * ROWS + 16 * half
-                    x_send[step, way, at : at + 16, :] = values.astype(jnp.bfloat16)
-            copy(step, way).start()
-        for way, number, plane, row in ((4, 7, 8, last - 7), (5, 8, 1, first), (6, 9, 8, first), (7, 10, 1, last - 7)):
-            c_send[step, way - 4] = post[plane, number, row : row + 8, :]
-            copy(step, way).start()
-
-    def send_y(step, post):
-        for way, row, group in ((2, last, UP), (3, first, DOWN)):
-            for place, number in enumerate(group):
-                for plane in range(8):
-                    at = place * 8 + plane
-                    y_send[step, way - 2, at : at + 1, :] = post[plane + 1, number, row : row + 1, :]
-            copy(step, way).start()
-
-    def receive(step, post):
-        for way in range(8):
-            copy(step, way).wait_recv()
-        for way, plane, group in ((0, 0, RIGHT), (1, 9, LEFT)):
-            for place, number in enumerate(group):
-                for half in range(2):
-                    at = place * ROWS + 16 * half
-                    values = x_recv[step, way, at : at + 16, :]
-                    post[plane, number, first + 16 * half : first + 16 * half + 16, :] = values.astype(jnp.float32)
-        for way, row, group in ((2, first - 1, UP), (3, last + 1, DOWN)):
-            for place, number in enumerate(group):
-                for plane in range(8):
-                    at = place * 8 + plane
-                    post[plane + 1, number, row : row + 1, :] = y_recv[step, way - 2, at : at + 1, :]
-        for way, number, plane, row, at in (
-            (4, 7, 0, first - 1, 7),
-            (5, 8, 9, last + 1, 0),
-            (6, 9, 0, last + 1, 0),
-            (7, 10, 9, first - 1, 7),
-        ):
-            post[plane, number, row : row + 1, :] = c_recv[step, way - 4, at : at + 1, :]
-
-    def work(step, plane, tile):
-        if step == 0:
+                    rows = start[number, pl.ds(128 * half + first + plane, 16, stride=8), :]
+                    x_send[way, plane, number, 16 * half : 16 * half + 16, :] = rows.astype(jnp.bfloat16)
+        y_send[0, number] = start[number, 8 * ROWS - 16 : 8 * ROWS, :].astype(jnp.bfloat16)
+        y_send[1, number] = start[number, 0:16, :].astype(jnp.bfloat16)
+        return carry
+
+    lax.fori_loop(0, POPS, population, 0)
+
+
+def lattice(
+    start, solid, result, partners, posts, fx_send, fx_recv, fy_send, fy_recv, f_sent, f_came,
+    sy_send, sy_recv, s_sent, s_came, f_edge, s_edge,
+):
+    def start_halo(way):
+        return start_copy(way, partners, fx_send, fx_recv, fy_send, fy_recv, f_sent, f_came)
+
+    def solid_halo(way):
+        return solid_copy(way, partners, solid, sy_send, sy_recv, s_sent, s_came)
+
+    for way in range(8):
+        solid_halo(way).start()
+
+    def begin(plane, carry):
+        for tile in range(4):
             f = [start[i, pl.ds(64 * tile + plane, 8, stride=8), :] for i in range(POPS)]
-        else:
-            f = pull_all(posts.at[(step - 1) % 2], plane, tile)
+            post = collide(f, solid[plane + WIDE, 8 * tile : 8 * tile + 8, :])
+            for i in range(POPS):
+                posts[0, plane + WIDE, i, TOP + 8 * tile : TOP + 8 * tile + 8, :] = post[i]
+        return carry
+
+    def reader(source, plane, tile):
+        base = TOP + 8 * tile
+        return lambda number, shift_x, down: source[plane - shift_x, number, base + down : base + down + 8, :]
+
+    def advance(step, plane, tile):
+        f = pull_all(reader(posts.at[(step - 1) % 2], plane, tile))
         post = collide(f, solid[plane, 8 * tile : 8 * tile + 8, :])
-        base = TOP + 8 * tile
         for i in range(POPS):
-            posts[step % 2, plane + 1, i, base : base + 8, :] = post[i]
-
-    def inner(step):
-        def planes(plane, carry):
-            for tile in (1, 2):
-                work(step, plane, tile)
+            posts[step % 2, plane, i, TOP + 8 * tile : TOP + 8 * tile + 8, :] = post[i]
+
+    def planes_of(step, first, last, tiles):
+        def body(plane, carry):
+            for tile in tiles:
+                advance(step, plane, tile)
             return carry
 
-        lax.fori_loop(1, 7, planes, 0)
-
-    def outer(step):
-        post = posts.at[step % 2]
-
-        def sides(side, carry):
-            for tile in range(4):
-                work(step, side * 7, tile)
-            return carry
-
-        lax.fori_loop(0, 2, sides, 0)
-        send_x(step, post)
-
-        def edges(plane, carry):
-            for tile in (0, 3):
-                work(step, plane, tile)
-            return carry
-
-        lax.fori_loop(1, 7, edges, 0)
-        send_y(step, post)
-
-    outer(0)
-    inner(0)
-    for step in range(1, STEPS):
-        inner(step)
-        receive(step - 1, posts.at[(step - 1) % 2])
-        outer(step)
-    post = posts.at[(STEPS - 1) % 2]
-
-    def finish(numbers):
-        def planes(plane, carry):
-            for tile in range(4):
-                at = pl.ds(64 * tile + plane, 8, stride=8)
-                for number in numbers:
-                    if number == 0:
-                        result[0, at, :] = pull(post, 0, plane, tile)
-                    else:
-                        result[number, at, :], result[number + 1, at, :] = pull_pair(post, number, plane, tile)
-            return carry
-
-        lax.fori_loop(0, 8, planes, 0)
-
-    finish(UNSHIFTED)
-    receive(STEPS - 1, post)
-    finish([number for number in range(1, POPS, 2) if number not in UNSHIFTED])
-    for step in range(STEPS):
-        for way in range(8):
-            copy(step, way).wait_send()
+        lax.fori_loop(first, last, body, 0)
+
+    def flat(step):
+        return posts.at[step % 2].reshape(PLANES * POPS * TALL, LANES)
+
+    def edge_rows(row, plane, number):
+        return pl.ds((plane * POPS + number) * TALL + row, 8, stride=POPS * TALL)
+
+    def edge(step, row, first):
+        source, landing = flat(step - 1), flat(step)
+        f = pull_all(lambda number, shift_x, down: source[edge_rows(row + down, first - shift_x, number), :])
+        post = collide(f, s_edge[1 if row < TOP else 2, first : first + 8, :])
+        for i in range(POPS):
+            landing[edge_rows(row, first, i), :] = post[i]
+
+    lax.fori_loop(0, 8, begin, 0)
+    planes_of(1, 4, 10, (1, 2))
+
+    for way in range(8):
+        start_halo(way).wait_recv()
+
+    def spread(number, carry):
+        for side, ways in enumerate(HALO_WAYS):
+            middle, below, above = [fy_recv[way - 2, number].astype(jnp.float32) for way in ways]
+            for pair in range(2):
+                f_edge[number, 2 * side + pair, WIDE : WIDE + 8, :] = middle[8 * pair : 8 * pair + 8]
+                f_edge[number, 2 * side + pair, 0:WIDE, :] = below[8 * pair + 8 - WIDE : 8 * pair + 8]
+                f_edge[number, 2 * side + pair, WIDE + 8 : PLANES, :] = above[8 * pair : 8 * pair + WIDE]
+        return carry
+
+    lax.fori_loop(0, POPS, spread, 0)
+    for way in range(8):
+        solid_halo(way).wait_recv()
+    for side, ways in enumerate(HALO_WAYS):
+        middle, below, above = [sy_recv[way - 2] for way in ways]
+        for pair in range(2):
+            s_edge[2 * side + pair, WIDE : WIDE + 8, :] = middle[8 * pair : 8 * pair + 8]
+            s_edge[2 * side + pair, 0:WIDE, :] = below[8 * pair + 8 - WIDE : 8 * pair + 8]
+            s_edge[2 * side + pair, WIDE + 8 : PLANES, :] = above[8 * pair : 8 * pair + WIDE]
+
+    def begin_beside(plane, carry):
+        for side in range(2):
+            at = plane + side * (8 + WIDE)
+            for half in range(2):
+                f = [fx_recv[side, plane, i, 16 * half : 16 * half + 16, :].astype(jnp.float32) for i in range(POPS)]
+                post = collide(f, solid[at, 16 * half : 16 * half + 16, :])
+                for i in range(POPS):
+                    posts[0, at, i, TOP + 16 * half : TOP + 16 * half + 16, :] = post[i]
+        return carry
+
+    lax.fori_loop(0, WIDE, begin_beside, 0)
+    for place, row in enumerate((TOP - 2, TOP - 1, TOP + ROWS, TOP + ROWS + 1)):
+        for first in (0, PLANES - 8):
+            f = [f_edge[i, place, first : first + 8, :] for i in range(POPS)]
+            post = collide(f, s_edge[place, first : first + 8, :])
+            for i in range(POPS):
+                flat(0)[edge_rows(row, first, i), :] = post[i]
+    planes_of(1, 1, 4, range(4))
+    planes_of(1, 10, 13, range(4))
+    planes_of(1, 4, 10, (0, 3))
+    for row in (TOP - 1, TOP + ROWS):
+        for first in (1, 5):
+            edge(1, row, first)
+    planes_of(2, 2, 12, range(4))
+    for row in (TOP - 1, TOP + ROWS):
+        for first in (2, 4):
+            edge(2, row, first)
+
+    def finish(plane, carry):
+        for tile in range(4):
+            at = pl.ds(64 * tile + plane, 8, stride=8)
+            read = reader(posts.at[0], plane + WIDE, tile)
+            result[0, at, :] = pull(read, 0)
+            for number in range(1, POPS, 2):
+                result[number, at, :], result[number + 1, at, :] = pull_pair(read, number)
+        return carry
+
+    lax.fori_loop(0, 8, finish, 0)
+    for way in range(8):
+        start_halo(way).wait_send()
+        solid_halo(way).wait_send()
 
 
 def lattice_scratch():
     return [
-        pltpu.VMEM((2, 10, POPS, TALL, LANES), jnp.float32),
-        pltpu.VMEM((STEPS, 2, 5 * ROWS, LANES), jnp.bfloat16),
-        pltpu.VMEM((STEPS, 2, 5 * ROWS, LANES), jnp.bfloat16),
-        pltpu.VMEM((STEPS, 2, 40, LANES), jnp.float32),
-        pltpu.VMEM((STEPS, 2, 40, LANES), jnp.float32),
-        pltpu.VMEM((STEPS, 4, 8, LANES), jnp.float32),
-        pltpu.VMEM((STEPS, 4, 8, LANES), jnp.float32),
-        pltpu.SemaphoreType.DMA((STEPS, 8)),
-        pltpu.SemaphoreType.DMA((STEPS, 8)),
+        pltpu.VMEM((2, PLANES, POPS, TALL, LANES), jnp.float32),
+        pltpu.VMEM((2, WIDE, POPS, ROWS, LANES), jnp.bfloat16),
+        pltpu.VMEM((2, WIDE, POPS, ROWS, LANES), jnp.bfloat16),
+        pltpu.VMEM((2, POPS, 16, LANES), jnp.bfloat16),
+        pltpu.VMEM((6, POPS, 16, LANES), jnp.bfloat16),
+        pltpu.SemaphoreType.DMA((8,)),
+        pltpu.SemaphoreType.DMA((8,)),
+        pltpu.VMEM((2, 16, LANES), jnp.float32),
+        pltpu.VMEM((6, 16, LANES), jnp.float32),
+        pltpu.SemaphoreType.DMA((8,)),
+        pltpu.SemaphoreType.DMA((8,)),
+        pltpu.VMEM((POPS, 4, 16, LANES), jnp.float32),
+        pltpu.VMEM((4, 16, LANES), jnp.float32),
     ]
 
 
@@ -375,6 +413,8 @@
     target_ref, count_ref, cell_ref, weight_ref, start, operand, outgoing, arrived, total, solid,
     load_sem, sent_sem, arrived_sem, *lattice_refs,
 ):
+    posts, fx_send, fx_recv, fy_send, fy_recv, f_sent, f_came, sy_send = lattice_refs[:8]
+    partners = partner_devices()
     me = lax.axis_index("gx") * along_y + lax.axis_index("gy")
     sources = (target_hbm, count_hbm, cell_hbm, weight_hbm, start_hbm)
     landings = (target_ref, count_ref, cell_ref, weight_ref, start)
@@ -397,6 +437,8 @@
         load.wait()
     slot_row = brick_slots(me, bricks, target_ref, count_ref, cell_ref, weight_ref, operand)
     gather_slots(me, bricks, slot_row, operand, outgoing)
+    loads[4].wait()
+    pack_start(start, fx_send, fy_send)
     total[...] = jnp.zeros_like(total)
     pl.semaphore_wait(barrier, bricks - 1)
 
@@ -412,6 +454,8 @@
         return carry
 
     lax.fori_loop(1, bricks, send, 0)
+    for way in range(8):
+        start_copy(way, partners, fx_send, fx_recv, fy_send, fy_recv, f_sent, f_came).start()
     arrived[0] = outgoing[0]
 
     def add(group):
@@ -451,10 +495,11 @@
     for plane in range(8):
         for tile in range(4):
             piece = fraction[plane * ROWS + 8 * tile : plane * ROWS + 8 * tile + 8, :]
-            solid[plane, 8 * tile : 8 * tile + 8, :] = piece
+            solid[plane + WIDE, 8 * tile : 8 * tile + 8, :] = piece
             solid_ref[pl.ds(64 * tile + plane, 8, stride=8), :] = piece
-    loads[4].wait()
-    lattice(start, solid, result, *lattice_refs)
+    sy_send[0] = solid_ref[8 * ROWS - 16 : 8 * ROWS, :]
+    sy_send[1] = solid_ref[0:16, :]
+    lattice(start, solid, result, partners, *lattice_refs)
     everything = outgoing.at[pl.ds(1, bricks - 1)]
     pltpu.make_async_copy(everything, everything, sent_sem).wait()
 
@@ -492,7 +537,7 @@
             pltpu.VMEM((bricks, 8, LANES), jnp.int32),
             pltpu.VMEM((bricks, 8, LANES), jnp.int32),
             pltpu.VMEM((8 * ROWS, 2 * LANES), jnp.float32),
-            pltpu.VMEM((8, ROWS, LANES), jnp.float32),
+            pltpu.VMEM((PLANES, ROWS, LANES), jnp.float32),
             pltpu.SemaphoreType.DMA((5,)),
             pltpu.SemaphoreType.DMA,
             pltpu.SemaphoreType.DMA((bricks // GROUP,)),

time: 51.5 us -> 59.3 us (1.15)
  the two profiles are of different devices: /device:TPU:1 before, /device:TPU:13 now
where the time goes in v5:
time: 59.3 us; the launch traced here: 59.2 us
  Pallas kernels  56.5 us (95%)
  local copies, waits for them, and re-layouts  2.11 us (4%)
  between operations  0.64 us (1%)
    pallas_call x1, Pallas kernels, on_device(): pl.pallas_call(functools.partial(program_kernel, bricks, along_y), out_sh...  56.5 us
    unnamed x2, local copies, waits for them, and re-layouts  2.11 us

profile of v5, /device:TPU:13, one launch (start us, length us, event | category | flops | bytes accessed | tf_op | source)
XLA Modules:
  0.0 59.2 jit_solution(6580199397403267106)
XLA Ops:
  0.6 56.5 %permeability.1 = (f32[256,128]{1,0:T(8,128)S(1)}, f32[19,256,128]{2,1,0:T(8,128)S(1)}) custom-call(s32[1,384]{1,0:T(1,128)} %bitcast.19, s32[384]{0:T(512)} %count_hbm.1, s32[384,256]{1,0:T(8,128)} %cell_hbm.1, bf16[384,256]{1,0:T(8,128)(2,1)} %weight_hbm.1, f32[19,256,128]{2,1,0:T(8,128)} %bitcast.18), custom_call_target="tpu_custom_call" | custom-call | tf_op jit(solution)/shard_map/permeability/pallas_call | solution.py:522
  57.1 1.5 %copy.9 = f32[19,8,4096]{2,1,0:T(8,128)} copy(f32[19,8,4096]{2,1,0:T(8,128)S(1)} %bitcast.16) | data formatting | bytes 4980736
  58.6 0.7 %copy.10 = f32[8,4096]{1,0:T(8,128)} copy(f32[8,4096]{1,0:T(8,128)S(1)} %bitcast.17) | data formatting | bytes 262144

commit v6 on v5

--- a/solution.py
+++ b/solution.py
@@ -49,40 +49,38 @@
 TOP = 8
 TALL = 48
 POPS = 19
+RIGHT = (1, 7, 9, 11, 13)
+LEFT = (2, 8, 10, 12, 14)
 WIDE = STEPS
+NEAR = WIDE - 1
 PLANES = 8 + 2 * WIDE
 
 
 def pull(read, number):
     shift_x, shift_y, shift_z = lattice_velocities[number]
-    even = lax.broadcasted_iota(jnp.int32, (8, LANES), 1) < NZ
+    lane = lax.broadcasted_iota(jnp.int32, (8, LANES), 1)
+    even, z_place = lane < NZ, lane & (NZ - 1)
     values = read(number, shift_x, 0)
-    turn = shift_z
+    turn = 0
     if shift_y == 1:
         values = jnp.where(even, values, read(number, shift_x, -1))
-        turn += NZ
+        turn = NZ
     if shift_y == -1:
         values = jnp.where(even, read(number, shift_x, 1), values)
-        turn += NZ
-    return pltpu.roll(values, turn % LANES, 1) if turn else values
+        turn = NZ
+    if shift_z == 0:
+        return pltpu.roll(values, turn, 1) if turn else values
+    near = pltpu.roll(values, (shift_z + turn) % LANES, 1)
+    wrapped = pltpu.roll(values, (shift_z + NZ + turn) % LANES, 1)
+    return jnp.where(z_place == (0 if shift_z == 1 else NZ - 1), wrapped, near)
 
 
 def pull_pair(read, number):
-    pair = [pull(read, number), pull(read, number + 1)]
-    shift_z = lattice_velocities[number][2]
-    if shift_z == 0:
-        return pair
-    z_place = lax.broadcasted_iota(jnp.int32, (8, LANES), 1) & (NZ - 1)
-    edge, other = (0, NZ - 1) if shift_z == 1 else (NZ - 1, 0)
-    turned = pltpu.roll(jnp.where(z_place == edge, pair[0], pair[1]), NZ, 1)
-    return [jnp.where(z_place == edge, turned, pair[0]), jnp.where(z_place == other, turned, pair[1])]
+    return [pull(read, number), pull(read, number + 1)]
 
 
 def pull_all(read):
-    values = [pull(read, 0)]
-    for number in range(1, POPS, 2):
-        values += pull_pair(read, number)
-    return values
+    return [pull(read, number) for number in range(POPS)]
 
 
 def collide(f, solid):
@@ -158,9 +156,9 @@
 
 def solid_copy(way, partners, solid, y_send, y_recv, sent, came):
     if way == 0:
-        source, landing = solid.at[pl.ds(8, WIDE)], solid.at[pl.ds(0, WIDE)]
+        source, landing = solid.at[pl.ds(9, NEAR)], solid.at[pl.ds(1, NEAR)]
     elif way == 1:
-        source, landing = solid.at[pl.ds(WIDE, WIDE)], solid.at[pl.ds(8 + WIDE, WIDE)]
+        source, landing = solid.at[pl.ds(WIDE, NEAR)], solid.at[pl.ds(8 + WIDE, NEAR)]
     else:
         source, landing = y_send.at[SIDE[way]], y_recv.at[way - 2]
     return pltpu.make_async_remote_copy(
@@ -171,8 +169,8 @@
 
 def pack_start(start, x_send, y_send):
     def population(number, carry):
-        for way, first in ((0, 8 - WIDE), (1, 0)):
-            for plane in range(WIDE):
+        for way, first in ((0, 8 - NEAR), (1, 0)):
+            for plane in range(NEAR):
                 for half in range(2):
                     rows = start[number, pl.ds(128 * half + first + plane, 16, stride=8), :]
                     x_send[way, plane, number, 16 * half : 16 * half + 16, :] = rows.astype(jnp.bfloat16)
@@ -184,9 +182,11 @@
 
 
 def lattice(
-    start, solid, result, partners, posts, fx_send, fx_recv, fy_send, fy_recv, f_sent, f_came,
-    sy_send, sy_recv, s_sent, s_came, f_edge, s_edge,
+    start, solid, result, partners, even_posts, odd_posts, even_stage, odd_stage, fx_send, fx_recv, fy_send, fy_recv, f_sent, f_came,
+    sy_send, sy_recv, s_sent, s_came, f_edge, s_edge, far_send, far_recv, far_sent, far_came,
 ):
+    posts = (even_posts, odd_posts)
+
     def start_halo(way):
         return start_copy(way, partners, fx_send, fx_recv, fy_send, fy_recv, f_sent, f_came)
 
@@ -201,29 +201,41 @@
             f = [start[i, pl.ds(64 * tile + plane, 8, stride=8), :] for i in range(POPS)]
             post = collide(f, solid[plane + WIDE, 8 * tile : 8 * tile + 8, :])
             for i in range(POPS):
-                posts[0, plane + WIDE, i, TOP + 8 * tile : TOP + 8 * tile + 8, :] = post[i]
+                posts[0][plane + WIDE, i, TOP + 8 * tile : TOP + 8 * tile + 8, :] = post[i]
         return carry
 
     def reader(source, plane, tile):
         base = TOP + 8 * tile
         return lambda number, shift_x, down: source[plane - shift_x, number, base + down : base + down + 8, :]
 
-    def advance(step, plane, tile):
-        f = pull_all(reader(posts.at[(step - 1) % 2], plane, tile))
-        post = collide(f, solid[plane, 8 * tile : 8 * tile + 8, :])
-        for i in range(POPS):
-            posts[step % 2, plane, i, TOP + 8 * tile : TOP + 8 * tile + 8, :] = post[i]
+    def fetch(step, plane, tiles, stage):
+        for tile in tiles:
+            f = pull_all(reader(posts[(step - 1) % 2], plane, tile))
+            for i in range(POPS):
+                stage[tile, i] = f[i]
+
+    def settle(step, plane, tiles, stage):
+        for tile in tiles:
+            post = collide([stage[tile, i] for i in range(POPS)], solid[plane, 8 * tile : 8 * tile + 8, :])
+            for i in range(POPS):
+                posts[step % 2][plane, i, TOP + 8 * tile : TOP + 8 * tile + 8, :] = post[i]
 
     def planes_of(step, first, last, tiles):
-        def body(plane, carry):
-            for tile in tiles:
-                advance(step, plane, tile)
+        def body(pair, carry):
+            plane = first + 2 * pair
+            fetch(step, plane + 1, tiles, odd_stage)
+            settle(step, plane, tiles, even_stage)
+            fetch(step, jnp.minimum(plane + 2, last - 1), tiles, even_stage)
+            settle(step, plane + 1, tiles, odd_stage)
             return carry
 
-        lax.fori_loop(first, last, body, 0)
+        fetch(step, first, tiles, even_stage)
+        lax.fori_loop(0, (last - first) // 2, body, 0)
+        if (last - first) % 2:
+            settle(step, last - 1, tiles, even_stage)
 
     def flat(step):
-        return posts.at[step % 2].reshape(PLANES * POPS * TALL, LANES)
+        return posts[step % 2].reshape(PLANES * POPS * TALL, LANES)
 
     def edge_rows(row, plane, number):
         return pl.ds((plane * POPS + number) * TALL + row, 8, stride=POPS * TALL)
@@ -235,7 +247,21 @@
         for i in range(POPS):
             landing[edge_rows(row, first, i), :] = post[i]
 
-    lax.fori_loop(0, 8, begin, 0)
+    def far_copy(way):
+        return pltpu.make_async_remote_copy(
+            src_ref=far_send.at[way], dst_ref=far_recv.at[way], send_sem=far_sent.at[way], recv_sem=far_came.at[way],
+            device_id=partners[way], device_id_type=MESH,
+        )
+
+    lax.fori_loop(0, 2, lambda side, carry: begin(8 - WIDE - side * (8 - 2 * WIDE + 1), carry), 0)
+    for way, plane, group in ((0, 8, RIGHT), (1, 2 * WIDE - 1, LEFT)):
+        for place, number in enumerate(group):
+            for half in range(2):
+                rows = posts[0][plane, number, TOP + 16 * half : TOP + 16 * half + 16, :]
+                at = place * ROWS + 16 * half
+                far_send[way, at : at + 16, :] = rows.astype(jnp.bfloat16)
+        far_copy(way).start()
+    lax.fori_loop(0, 6, lambda place, carry: begin(place + lax.div(place, 2), carry), 0)
     planes_of(1, 4, 10, (1, 2))
 
     for way in range(8):
@@ -262,15 +288,22 @@
 
     def begin_beside(plane, carry):
         for side in range(2):
-            at = plane + side * (8 + WIDE)
+            at = plane + (1 if side == 0 else 8 + WIDE)
             for half in range(2):
                 f = [fx_recv[side, plane, i, 16 * half : 16 * half + 16, :].astype(jnp.float32) for i in range(POPS)]
                 post = collide(f, solid[at, 16 * half : 16 * half + 16, :])
                 for i in range(POPS):
-                    posts[0, at, i, TOP + 16 * half : TOP + 16 * half + 16, :] = post[i]
-        return carry
-
-    lax.fori_loop(0, WIDE, begin_beside, 0)
+                    posts[0][at, i, TOP + 16 * half : TOP + 16 * half + 16, :] = post[i]
+        return carry
+
+    lax.fori_loop(0, NEAR, begin_beside, 0)
+    for way, plane, group in ((0, 0, RIGHT), (1, PLANES - 1, LEFT)):
+        far_copy(way).wait_recv()
+        for place, number in enumerate(group):
+            for half in range(2):
+                at = place * ROWS + 16 * half
+                rows = far_recv[way, at : at + 16, :]
+                posts[0][plane, number, TOP + 16 * half : TOP + 16 * half + 16, :] = rows.astype(jnp.float32)
     for place, row in enumerate((TOP - 2, TOP - 1, TOP + ROWS, TOP + ROWS + 1)):
         for first in (0, PLANES - 8):
             f = [f_edge[i, place, first : first + 8, :] for i in range(POPS)]
@@ -291,7 +324,7 @@
     def finish(plane, carry):
         for tile in range(4):
             at = pl.ds(64 * tile + plane, 8, stride=8)
-            read = reader(posts.at[0], plane + WIDE, tile)
+            read = reader(posts[0], plane + WIDE, tile)
             result[0, at, :] = pull(read, 0)
             for number in range(1, POPS, 2):
                 result[number, at, :], result[number + 1, at, :] = pull_pair(read, number)
@@ -301,13 +334,18 @@
     for way in range(8):
         start_halo(way).wait_send()
         solid_halo(way).wait_send()
+    for way in range(2):
+        far_copy(way).wait_send()
 
 
 def lattice_scratch():
     return [
-        pltpu.VMEM((2, PLANES, POPS, TALL, LANES), jnp.float32),
-        pltpu.VMEM((2, WIDE, POPS, ROWS, LANES), jnp.bfloat16),
-        pltpu.VMEM((2, WIDE, POPS, ROWS, LANES), jnp.bfloat16),
+        pltpu.VMEM((PLANES, POPS, TALL, LANES), jnp.float32),
+        pltpu.VMEM((PLANES, POPS, TALL, LANES), jnp.float32),
+        pltpu.VMEM((4, POPS, 8, LANES), jnp.float32),
+        pltpu.VMEM((4, POPS, 8, LANES), jnp.float32),
+        pltpu.VMEM((2, NEAR, POPS, ROWS, LANES), jnp.bfloat16),
+        pltpu.VMEM((2, NEAR, POPS, ROWS, LANES), jnp.bfloat16),
         pltpu.VMEM((2, POPS, 16, LANES), jnp.bfloat16),
         pltpu.VMEM((6, POPS, 16, LANES), jnp.bfloat16),
         pltpu.SemaphoreType.DMA((8,)),
@@ -318,6 +356,10 @@
         pltpu.SemaphoreType.DMA((8,)),
         pltpu.VMEM((POPS, 4, 16, LANES), jnp.float32),
         pltpu.VMEM((4, 16, LANES), jnp.float32),
+        pltpu.VMEM((2, 5 * ROWS, LANES), jnp.bfloat16),
+        pltpu.VMEM((2, 5 * ROWS, LANES), jnp.bfloat16),
+        pltpu.SemaphoreType.DMA((2,)),
+        pltpu.SemaphoreType.DMA((2,)),
     ]
 
 
@@ -413,7 +455,7 @@
     target_ref, count_ref, cell_ref, weight_ref, start, operand, outgoing, arrived, total, solid,
     load_sem, sent_sem, arrived_sem, *lattice_refs,
 ):
-    posts, fx_send, fx_recv, fy_send, fy_recv, f_sent, f_came, sy_send = lattice_refs[:8]
+    fx_send, fx_recv, fy_send, fy_recv, f_sent, f_came, sy_send = lattice_refs[4:11]
     partners = partner_devices()
     me = lax.axis_index("gx") * along_y + lax.axis_index("gy")
     sources = (target_hbm, count_hbm, cell_hbm, weight_hbm, start_hbm)
@@ -454,8 +496,6 @@
         return carry
 
     lax.fori_loop(1, bricks, send, 0)
-    for way in range(8):
-        start_copy(way, partners, fx_send, fx_recv, fy_send, fy_recv, f_sent, f_came).start()
     arrived[0] = outgoing[0]
 
     def add(group):
@@ -485,6 +525,11 @@
         @pl.when(group > 0)
         def _():
             landed(group, 0)
+
+        @pl.when(group == 0)
+        def _():
+            for way in range(8):
+                start_copy(way, partners, fx_send, fx_recv, fy_send, fy_recv, f_sent, f_came).start()
 
         add(group)
         return carry

time: 59.3 us -> 43.9 us (0.74)
  the two profiles are of different devices: /device:TPU:13 before, /device:TPU:1 now
where the time goes in v6:
time: 43.9 us; the launch traced here: 43.8 us
  Pallas kernels  41.1 us (94%)
  local copies, waits for them, and re-layouts  2.11 us (5%)
  between operations  0.64 us (1%)
    pallas_call x1, Pallas kernels, on_device(): pl.pallas_call(functools.partial(program_kernel, bricks, along_y), out_sh...  41.1 us
    unnamed x2, local copies, waits for them, and re-layouts  2.11 us

profile of v6, /device:TPU:1, one launch (start us, length us, event | category | flops | bytes accessed | tf_op | source)
XLA Modules:
  0.0 43.8 jit_solution(5730929770700483159)
XLA Ops:
  0.6 41.1 %permeability.1 = (f32[256,128]{1,0:T(8,128)S(1)}, f32[19,256,128]{2,1,0:T(8,128)S(1)}) custom-call(s32[1,384]{1,0:T(1,128)} %bitcast.19, s32[384]{0:T(512)} %count_hbm.1, s32[384,256]{1,0:T(8,128)} %cell_hbm.1, bf16[384,256]{1,0:T(8,128)(2,1)} %weight_hbm.1, f32[19,256,128]{2,1,0:T(8,128)} %bitcast.18), custom_call_target="tpu_custom_call" | custom-call | tf_op jit(solution)/shard_map/permeability/pallas_call | solution.py:567
  41.7 1.5 %copy.9 = f32[19,8,4096]{2,1,0:T(8,128)} copy(f32[19,8,4096]{2,1,0:T(8,128)S(1)} %bitcast.16) | data formatting | bytes 4980736
  43.1 0.7 %copy.10 = f32[8,4096]{1,0:T(8,128)} copy(f32[8,4096]{1,0:T(8,128)S(1)} %bitcast.17) | data formatting | bytes 262144

commit v7 on v6

--- a/solution.py
+++ b/solution.py
@@ -181,8 +181,13 @@
     lax.fori_loop(0, POPS, population, 0)
 
 
+def reader(source, plane, tile):
+    base = TOP + 8 * tile
+    return lambda number, shift_x, down: source[plane - shift_x, number, base + down : base + down + 8, :]
+
+
 def lattice(
-    start, solid, result, partners, even_posts, odd_posts, even_stage, odd_stage, fx_send, fx_recv, fy_send, fy_recv, f_sent, f_came,
+    start, solid, even_posts, partners, odd_posts, even_stage, odd_stage, fx_send, fx_recv, fy_send, fy_recv, f_sent, f_came,
     sy_send, sy_recv, s_sent, s_came, f_edge, s_edge, far_send, far_recv, far_sent, far_came,
 ):
     posts = (even_posts, odd_posts)
@@ -203,10 +208,6 @@
             for i in range(POPS):
                 posts[0][plane + WIDE, i, TOP + 8 * tile : TOP + 8 * tile + 8, :] = post[i]
         return carry
-
-    def reader(source, plane, tile):
-        base = TOP + 8 * tile
-        return lambda number, shift_x, down: source[plane - shift_x, number, base + down : base + down + 8, :]
 
     def fetch(step, plane, tiles, stage):
         for tile in tiles:
@@ -321,16 +322,6 @@
         for first in (2, 4):
             edge(2, row, first)
 
-    def finish(plane, carry):
-        for tile in range(4):
-            at = pl.ds(64 * tile + plane, 8, stride=8)
-            read = reader(posts[0], plane + WIDE, tile)
-            result[0, at, :] = pull(read, 0)
-            for number in range(1, POPS, 2):
-                result[number, at, :], result[number + 1, at, :] = pull_pair(read, number)
-        return carry
-
-    lax.fori_loop(0, 8, finish, 0)
     for way in range(8):
         start_halo(way).wait_send()
         solid_halo(way).wait_send()
@@ -340,7 +331,6 @@
 
 def lattice_scratch():
     return [
-        pltpu.VMEM((PLANES, POPS, TALL, LANES), jnp.float32),
         pltpu.VMEM((PLANES, POPS, TALL, LANES), jnp.float32),
         pltpu.VMEM((4, POPS, 8, LANES), jnp.float32),
         pltpu.VMEM((4, POPS, 8, LANES), jnp.float32),
@@ -451,11 +441,11 @@
 
 
 def program_kernel(
-    bricks, along_y, target_hbm, count_hbm, cell_hbm, weight_hbm, start_hbm, solid_ref, result,
+    bricks, along_y, target_hbm, count_hbm, cell_hbm, weight_hbm, start_hbm, solid_ref, even_posts,
     target_ref, count_ref, cell_ref, weight_ref, start, operand, outgoing, arrived, total, solid,
     load_sem, sent_sem, arrived_sem, *lattice_refs,
 ):
-    fx_send, fx_recv, fy_send, fy_recv, f_sent, f_came, sy_send = lattice_refs[4:11]
+    fx_send, fx_recv, fy_send, fy_recv, f_sent, f_came, sy_send = lattice_refs[3:10]
     partners = partner_devices()
     me = lax.axis_index("gx") * along_y + lax.axis_index("gy")
     sources = (target_hbm, count_hbm, cell_hbm, weight_hbm, start_hbm)
@@ -544,9 +534,49 @@
             solid_ref[pl.ds(64 * tile + plane, 8, stride=8), :] = piece
     sy_send[0] = solid_ref[8 * ROWS - 16 : 8 * ROWS, :]
     sy_send[1] = solid_ref[0:16, :]
-    lattice(start, solid, result, partners, *lattice_refs)
+    lattice(start, solid, even_posts, partners, *lattice_refs)
     everything = outgoing.at[pl.ds(1, bricks - 1)]
     pltpu.make_async_copy(everything, everything, sent_sem).wait()
+
+
+def stream_out_kernel(posts, solid_ref, result_hbm, solid_hbm, result, out_sem, solid_sem):
+    passing = pltpu.make_async_copy(solid_ref, solid_hbm, solid_sem)
+    passing.start()
+
+    def leave(tile):
+        rows = pl.ds(64 * tile, 64)
+        return pltpu.make_async_copy(result.at[:, rows], result_hbm.at[:, rows], out_sem.at[tile])
+
+    for tile in range(4):
+
+        def planes(pair, carry):
+            for plane in (2 * pair, 2 * pair + 1):
+                at = pl.ds(64 * tile + plane, 8, stride=8)
+                for number, values in enumerate(pull_all(reader(posts, plane + WIDE, tile))):
+                    result[number, at, :] = values
+            return carry
+
+        lax.fori_loop(0, 4, planes, 0)
+        leave(tile).start()
+    for tile in range(4):
+        leave(tile).wait()
+    passing.wait()
+
+
+def stream_out(posts, solid):
+    vmem, hbm = pl.BlockSpec(memory_space=pltpu.VMEM), pl.BlockSpec(memory_space=pltpu.HBM)
+    shape = jax.ShapeDtypeStruct((POPS, 8 * ROWS, LANES), jnp.float32)
+    return pl.pallas_call(
+        stream_out_kernel,
+        out_shape=(shape, jax.ShapeDtypeStruct(solid.shape, jnp.float32)),
+        in_specs=[vmem, vmem],
+        out_specs=(hbm, hbm),
+        scratch_shapes=[
+            pltpu.VMEM(shape.shape, jnp.float32), pltpu.SemaphoreType.DMA((4,)), pltpu.SemaphoreType.DMA
+        ],
+        compiler_params=pltpu.CompilerParams(vmem_limit_bytes=16 * 1024 * 1024),
+        name="stream_out",
+    )(pltpu.with_memory_space_constraint(posts, pltpu.VMEM), pltpu.with_memory_space_constraint(solid, pltpu.VMEM))
 
 
 def to_rows(values):
@@ -564,11 +594,11 @@
     bricks = lax.axis_size("gx") * along_y
     blocks, nodes = node_cell.shape
     vmem, hbm = pl.BlockSpec(memory_space=pltpu.VMEM), pl.BlockSpec(memory_space=pltpu.HBM)
-    solid, result = pl.pallas_call(
+    solid, posts = pl.pallas_call(
         functools.partial(program_kernel, bricks, along_y),
         out_shape=(
-            jax.ShapeDtypeStruct((8 * ROWS, LANES), jnp.float32),
-            jax.ShapeDtypeStruct((POPS, 8 * ROWS, LANES), jnp.float32),
+            pltpu.VMEM((8 * ROWS, LANES), jnp.float32),
+            pltpu.VMEM((PLANES, POPS, TALL, LANES), jnp.float32),
         ),
         in_specs=[hbm] * 5,
         out_specs=(vmem, vmem),
@@ -589,7 +619,7 @@
         ]
         + lattice_scratch(),
         compiler_params=pltpu.CompilerParams(
-            collective_id=0, has_side_effects=True, vmem_limit_bytes=48 * 1024 * 1024
+            collective_id=0, has_side_effects=True, vmem_limit_bytes=40 * 1024 * 1024
         ),
         name="permeability",
     )(
@@ -600,6 +630,7 @@
             )
         )
     )
+    result, solid = stream_out(posts, solid)
     return (from_rows(result), from_rows(solid))
 
 

time: 43.9 us -> 43.1 us (0.982)
  local copies, waits for them, and re-layouts: 2.11 us -> 0 us
  Pallas kernels: 41.1 us -> 42.4 us
    pallas_call x0 -> x1, Pallas kernels: none -> 2.84 us  [stream_out(): pl.pallas_call(stream_out_kernel, out_shape=(shape, jax.ShapeDtypeStruct(...]
    unnamed x2 -> x0, local copies, waits for them, and re-layouts: 2.11 us -> none
    pallas_call x1, Pallas kernels: 41.1 us -> 39.6 us  [on_device(): pl.pallas_call(functools.partial(program_kernel, bricks, along_y), out_sh...]
where the time goes in v7:
time: 43.1 us; the launch traced here: 43 us
  Pallas kernels  42.4 us (98%)
  between operations  0.64 us (1%)
    pallas_call x1, Pallas kernels, on_device(): pl.pallas_call(functools.partial(program_kernel, bricks, along_y), out_sh...  39.6 us
    pallas_call x1, Pallas kernels, stream_out(): pl.pallas_call(stream_out_kernel, out_shape=(shape, jax.ShapeDtypeStruct(...  2.84 us

profile of v7, /device:TPU:1, one launch (start us, length us, event | category | flops | bytes accessed | tf_op | source)
XLA Modules:
  0.0 43.0 jit_solution(16548651725350286638)
XLA Ops:
  0.6 39.6 %permeability.1 = (f32[256,128]{1,0:T(8,128)S(1)}, f32[14,19,48,128]{3,2,1,0:T(8,128)S(1)}) custom-call(s32[1,384]{1,0:T(1,128)} %bitcast.17, s32[384]{0:T(512)} %count_hbm.1, s32[384,256]{1,0:T(8,128)} %cell_hbm.1, bf16[384,256]{1,0:T(8,128)(2,1)} %weight_hbm.1, f32[19,256,128]{2,1,0:T(8,128)} %bitcast.16), custom_call_target="tpu_custom_call" | custom-call | tf_op jit(solution)/shard_map/permeability/pallas_call | solution.py:597
  40.2 2.8 %stream_out.1 = (f32[19,256,128]{2,1,0:T(8,128)}, f32[256,128]{1,0:T(8,128)}) custom-call(f32[14,19,48,128]{3,2,1,0:T(8,128)S(1)} %get-tuple-element.6.posts, f32[256,128]{1,0:T(8,128)S(1)} %get-tuple-element.7.solid_ref), custom_call_target="tpu_custom_call" | custom-call | tf_op jit(solution)/shard_map/stream_out/pallas_call | solution.py:569

commit v8 on v7

--- a/solution.py
+++ b/solution.py
@@ -353,7 +353,7 @@
     ]
 
 
-def brick_slots(me, bricks, target_ref, count_ref, cell_ref, weight_ref, operand):
+def brick_slots(bricks, target_ref, count_ref, cell_ref, weight_ref, operand):
     blocks, nodes = cell_ref.shape
     row = lax.broadcasted_iota(jnp.int32, (blocks, blocks), 0)
     col = lax.broadcasted_iota(jnp.int32, (blocks, blocks), 1)
@@ -382,13 +382,16 @@
     return slot_row
 
 
-def gather_slots(me, bricks, slot_row, operand, outgoing):
+def gather_slots(bricks, along_y, slot_row, operand, outgoing):
     rows = CHUNK * 8
+    here_x, here_y = lax.axis_index("gx"), lax.axis_index("gy")
     place = lax.broadcasted_iota(jnp.int32, (rows, 1), 0)
 
     def chunk_of(chunk, carry):
         offset = chunk * CHUNK + (place >> 3)
-        wanted = lax.rem(me + offset, bricks) * CAP + (place & (CAP - 1))
+        there_x = lax.rem(here_x + lax.div(offset, along_y), bricks // along_y)
+        there_y = lax.rem(here_y + lax.rem(offset, along_y), along_y)
+        wanted = (there_x * along_y + there_y) * CAP + (place & (CAP - 1))
         pick = jnp.where(wanted.astype(jnp.float32) == slot_row, 1.0, 0.0).astype(jnp.bfloat16)
         found = jnp.dot(pick, operand[...], preferred_element_type=jnp.float32)
         lower = (place & 7) < CAP
@@ -408,9 +411,19 @@
     lax.fori_loop(0, bricks // CHUNK, chunk_of, 0)
 
 
-def device_at(me, step, bricks, along_y):
-    target = lax.rem(me + step, bricks)
-    return lax.div(target, along_y), lax.rem(target, along_y)
+def for_each_partner(along_x, along_y, act):
+    here_x, here_y = lax.axis_index("gx"), lax.axis_index("gy")
+    there_y = [lax.rem(here_y + turn, along_y) for turn in range(along_y)]
+
+    def column(turn, carry):
+        there_x = lax.rem(here_x + turn, along_x)
+        for place in range(along_y):
+            act(turn * along_y + place, turn, (there_x, there_y[place]))
+        return carry
+
+    for place in range(1, along_y):
+        act(place, 0, (here_x, there_y[place]))
+    lax.fori_loop(1, along_x, column, 0)
 
 
 def one_hots(values, line):
@@ -447,7 +460,7 @@
 ):
     fx_send, fx_recv, fy_send, fy_recv, f_sent, f_came, sy_send = lattice_refs[3:10]
     partners = partner_devices()
-    me = lax.axis_index("gx") * along_y + lax.axis_index("gy")
+    along_x = bricks // along_y
     sources = (target_hbm, count_hbm, cell_hbm, weight_hbm, start_hbm)
     landings = (target_ref, count_ref, cell_ref, weight_ref, start)
     loads = [
@@ -458,34 +471,30 @@
         load.start()
     barrier = pltpu.get_barrier_semaphore()
 
-    def greet(step, carry):
-        pl.semaphore_signal(
-            barrier, inc=1, device_id=device_at(me, step, bricks, along_y), device_id_type=MESH
-        )
-        return carry
-
-    lax.fori_loop(1, bricks, greet, 0)
+    def greet(step, turn, device):
+        pl.semaphore_signal(barrier, inc=1, device_id=device, device_id_type=MESH)
+
+    for_each_partner(along_x, along_y, greet)
     for load in loads[:4]:
         load.wait()
-    slot_row = brick_slots(me, bricks, target_ref, count_ref, cell_ref, weight_ref, operand)
-    gather_slots(me, bricks, slot_row, operand, outgoing)
+    slot_row = brick_slots(bricks, target_ref, count_ref, cell_ref, weight_ref, operand)
+    gather_slots(bricks, along_y, slot_row, operand, outgoing)
     loads[4].wait()
     pack_start(start, fx_send, fy_send)
     total[...] = jnp.zeros_like(total)
     pl.semaphore_wait(barrier, bricks - 1)
 
-    def send(step, carry):
+    def send(step, turn, device):
         pltpu.make_async_remote_copy(
             src_ref=outgoing.at[step],
             dst_ref=arrived.at[step],
             send_sem=sent_sem,
-            recv_sem=arrived_sem.at[lax.div(step, GROUP)],
-            device_id=device_at(me, step, bricks, along_y),
+            recv_sem=arrived_sem.at[lax.div(turn, GROUP // along_y)],
+            device_id=device,
             device_id_type=MESH,
         ).start()
-        return carry
-
-    lax.fori_loop(1, bricks, send, 0)
+
+    for_each_partner(along_x, along_y, send)
     arrived[0] = outgoing[0]
 
     def add(group):

time: 43.1 us -> 43.1 us (level)
  no operation moved by 1% of the time
where the time goes in v8:
time: 43.1 us; the launch traced here: 43 us
  Pallas kernels  42.3 us (98%)
  between operations  0.64 us (1%)
    pallas_call x1, Pallas kernels, on_device(): pl.pallas_call(functools.partial(program_kernel, bricks, along_y), out_sh...  39.5 us
    pallas_call x1, Pallas kernels, stream_out(): pl.pallas_call(stream_out_kernel, out_shape=(shape, jax.ShapeDtypeStruct(...  2.84 us

profile of v8, /device:TPU:1, one launch (start us, length us, event | category | flops | bytes accessed | tf_op | source)
XLA Modules:
  0.0 43.0 jit_solution(13530029248344968324)
XLA Ops:
  0.6 39.5 %permeability.1 = (f32[256,128]{1,0:T(8,128)S(1)}, f32[14,19,48,128]{3,2,1,0:T(8,128)S(1)}) custom-call(s32[1,384]{1,0:T(1,128)} %bitcast.17, s32[384]{0:T(512)} %count_hbm.1, s32[384,256]{1,0:T(8,128)} %cell_hbm.1, bf16[384,256]{1,0:T(8,128)(2,1)} %weight_hbm.1, f32[19,256,128]{2,1,0:T(8,128)} %bitcast.16), custom_call_target="tpu_custom_call" | custom-call | tf_op jit(solution)/shard_map/permeability/pallas_call | solution.py:606
  40.1 2.8 %stream_out.1 = (f32[19,256,128]{2,1,0:T(8,128)}, f32[256,128]{1,0:T(8,128)}) custom-call(f32[14,19,48,128]{3,2,1,0:T(8,128)S(1)} %get-tuple-element.6.posts, f32[256,128]{1,0:T(8,128)S(1)} %get-tuple-element.7.solid_ref), custom_call_target="tpu_custom_call" | custom-call | tf_op jit(solution)/shard_map/stream_out/pallas_call | solution.py:578
